TPU v7x, 256 devices: a whole 4x4x8 slice. The times are simulated.
256 devices in a mesh: dp: 16 (over z, core), mp: 16 (over x, y).
Axes of the slice: x: 4, y: 4, z: 8, core: 2. Of those that a mesh axis runs over, the one named last changes fastest.
Arguments:
- item_tokens: bfloat16 [32768, 2048], P('dp', 'mp'), may hold values from -60 to 60
- gate_weight: bfloat16 [2048, 5632], P(None, 'mp'), may hold values from -0.125 to 0.125
- up_weight: bfloat16 [2048, 5632], P(None, 'mp'), may hold values from -0.125 to 0.125
- down_weight: bfloat16 [5632, 2048], P('mp'), may hold values from -0.078125 to 0.078125
- user_gain: float32 [2048], P('mp'), may hold values from 0.1 to 1.9
- query_weight: bfloat16 [2048, 2048], P(None, 'mp'), may hold values from -0.125 to 0.125
- key_weight: bfloat16 [2048, 256], replicated, may hold values from -0.125 to 0.125
- value_weight: bfloat16 [2048, 256], replicated, may hold values from -0.125 to 0.125
- out_weight: bfloat16 [2048, 2048], P('mp'), may hold values from -0.125 to 0.125
- item_slot: int32 [1024], P('dp'), may hold values from -1 to 4095, as said below
- lengths: int32 [16], P('dp'), may hold values from 16 to 256, as said below
- targets: int32 [4096], P('dp'), may hold values from -1 to 1023, as said below
Outputs:
- item_embeddings: bfloat16 [1024, 2048], P('dp', 'mp')
- user_states: bfloat16 [4096, 2048], P('dp', 'mp')
- losses: float32 [4096], P('dp')
Inputs may be any that keep to these rules, and one draw needn't show every extreme that they name: Slot item_slot[i] = h * 256 + p puts item i at position p of history h, or -1 if no history holds it. Slots are distinct and fill positions 0 to lengths[h] - 1 of every history. At most 64 items of one index of dp go to one history, and some history receives exactly 64 items from one index of dp. `lengths`: one history has exactly 256 items; the others have 16 to 32. targets[h * 256 + p] is the item at position p + 1 of history h, and -1 at the history's last position and past its end.
All inputs are finite; a program needn't handle non-finite values.
Results may differ from a plain program's by a relative error of at most 0.009.
Values may be sent and summed in bfloat16 or wider, within the bound.
A program may use at most 128 MiB of HBM per device.

v0:
```python
import jax
import jax.numpy as jnp
from jax import lax
from jax.sharding import PartitionSpec as P

D = 2048
HEADS = 32
KV_HEADS = 4
HEAD_DIM = 64
ITEM_TOK = 32


SCALE = 20.0


def rotate(values_in, positions):
    half_dim = values_in.shape[-1] // 2
    exponent = jnp.arange(half_dim, dtype=jnp.float32) * (2.0 / values_in.shape[-1])
    frequency = 10000.0 ** (-exponent)
    angles = positions.astype(jnp.float32)[:, None] * frequency[None, :]
    cosine = jnp.cos(angles)[:, None, :]
    sine_part = jnp.sin(angles)[:, None, :]
    first_half = values_in[..., :half_dim]
    second_half = values_in[..., half_dim:]
    return jnp.concatenate(
        [
            first_half * cosine - second_half * sine_part,
            second_half * cosine + first_half * sine_part,
        ],
        axis=-1,
    )


def local(
    item_tokens,
    gate_weight,
    up_weight,
    down_weight,
    user_gain,
    query_weight,
    key_weight,
    value_weight,
    out_weight,
    item_slot,
    lengths,
    targets,
):
    tok_rows = item_tokens.shape[0]
    item_count = tok_rows // ITEM_TOK
    feat_width = item_tokens.shape[1]
    shard_piece = lax.all_gather(item_tokens, "mp", axis=1, tiled=True)
    gate_acc = jnp.dot(shard_piece, gate_weight, preferred_element_type=jnp.float32)
    up_part = jnp.dot(shard_piece, up_weight, preferred_element_type=jnp.float32)
    hidden = (jax.nn.silu(gate_acc) * up_part).astype(jnp.bfloat16)
    mixed_rows = jnp.dot(hidden, down_weight, preferred_element_type=jnp.float32)
    tokens_wide = item_tokens.astype(jnp.float32)
    summed_share = lax.psum_scatter(mixed_rows, "mp", scatter_dimension=1, tiled=True)
    pooled = jnp.mean(
        (tokens_wide + summed_share).reshape(item_count, ITEM_TOK, feat_width), axis=1
    )
    item_embeddings = pooled.astype(jnp.bfloat16)
    all_items = lax.all_gather(item_embeddings, "dp", axis=0, tiled=True)
    all_wide = all_items.astype(jnp.float32)
    item_square = lax.psum(jnp.sum(all_wide * all_wide, axis=-1), "mp")
    item_unit = (all_wide * lax.rsqrt(item_square + 1e-06)[:, None]).astype(jnp.bfloat16)
    positions = targets.shape[0]
    own_index = lax.axis_index("dp")
    all_slots = lax.all_gather(item_slot, "dp", axis=0, tiled=True)
    held_here = (all_slots >= 0) & (all_slots // positions == own_index)
    place_int = jnp.where(held_here, all_slots % positions, positions)
    states = (
        jnp.zeros((positions, feat_width), jnp.bfloat16).at[place_int].set(all_items, mode="drop")
    )
    length = lengths[0]
    pos_ids = jnp.arange(positions, dtype=jnp.int32)
    states_wide = states.astype(jnp.float32)
    square_sum = lax.psum(jnp.sum(states_wide * states_wide, axis=-1), "mp")
    normed = (states_wide * lax.rsqrt(square_sum / D + 1e-05)[:, None] * user_gain).astype(
        jnp.bfloat16
    )
    mp_index = lax.axis_index("mp")
    local_heads = query_weight.shape[1] // HEAD_DIM
    kv_head = mp_index * local_heads // (HEADS // KV_HEADS)
    key_cols = lax.dynamic_slice_in_dim(key_weight, kv_head * HEAD_DIM, HEAD_DIM, 1)
    value_cols = lax.dynamic_slice_in_dim(value_weight, kv_head * HEAD_DIM, HEAD_DIM, 1)
    pair_cols = jnp.concatenate([key_cols, value_cols], axis=1)
    shard_piece = lax.all_gather(normed, "mp", axis=1, tiled=True)
    query_acc = jnp.dot(shard_piece, query_weight, preferred_element_type=jnp.float32)
    pair_acc = jnp.dot(shard_piece, pair_cols, preferred_element_type=jnp.float32)
    query_rot = rotate(query_acc.reshape(positions, local_heads, HEAD_DIM), pos_ids).astype(
        jnp.bfloat16
    )
    key_head = rotate(pair_acc[:, :HEAD_DIM].reshape(positions, 1, HEAD_DIM), pos_ids)[
        :, 0, :
    ].astype(jnp.bfloat16)
    value_head = pair_acc[:, HEAD_DIM:].astype(jnp.bfloat16)
    scores = jnp.einsum(
        "qhe,ke->hqk", query_rot, key_head, preferred_element_type=jnp.float32
    ) * HEAD_DIM ** (-0.5)
    allowed = (pos_ids[None, :] <= pos_ids[:, None]) & (pos_ids[None, :] < length)
    weights = jnp.where(allowed[None, :, :], jnp.exp(scores), 0.0)
    weights = (weights / jnp.sum(weights, axis=-1, keepdims=True)).astype(jnp.bfloat16)
    attended = jnp.einsum("hqk,ke->qhe", weights, value_head, preferred_element_type=jnp.float32)
    attended = attended.astype(jnp.bfloat16).reshape(positions, local_heads * HEAD_DIM)
    attn_rows = jnp.dot(attended, out_weight, preferred_element_type=jnp.float32)
    attn_share = lax.psum_scatter(
        attn_rows.astype(jnp.bfloat16), "mp", scatter_dimension=1, tiled=True
    ).astype(jnp.float32)
    valid_rows = (pos_ids < length).astype(jnp.float32)
    combined = (states_wide + attn_share) * valid_rows[:, None]
    user_states = combined.astype(jnp.bfloat16)
    user_square = lax.psum(jnp.sum(combined * combined, axis=-1), "mp")
    user_unit = (combined * lax.rsqrt(user_square + 1e-06)[:, None]).astype(jnp.bfloat16)
    partial_logits = jnp.einsum(
        "pd,jd->pj", user_unit, item_unit, preferred_element_type=jnp.float32
    )
    logits = SCALE * lax.psum(partial_logits.astype(jnp.bfloat16), "mp").astype(jnp.float32)
    columns = jnp.arange(logits.shape[1], dtype=jnp.int32)
    totals = jnp.sum(jnp.exp(logits), axis=-1)
    picked = jnp.sum(jnp.where(columns[None, :] == targets[:, None], logits, 0.0), axis=-1)
    losses = jnp.where(targets >= 0, jnp.log(totals) - picked, 0.0)
    return (item_embeddings, user_states, losses)


def solution(mesh):
    return jax.shard_map(
        local,
        mesh=mesh,
        in_specs=(
            P("dp", "mp"),
            P(None, "mp"),
            P(None, "mp"),
            P("mp", None),
            P("mp"),
            P(None, "mp"),
            P(),
            P(),
            P("mp", None),
            P("dp"),
            P("dp"),
            P("dp"),
        ),
        out_specs=(P("dp", "mp"), P("dp", "mp"), P("dp")),
        check_vma=False,
    )
```

profile of v0, /device:TPU:1, one launch (start us, length us, event | category | flops | bytes accessed | tf_op | source)
XLA Modules:
  0.0 565.8 jit_solution(235914686372290666)
XLA Ops:
  7.2 0.0 copy-start
  7.2 0.0 all-gather.3.cloned.1.call-start
  7.2 0.7 all-gather.3.cloned.1.call-update
  7.9 0.0 reduce-scatter.5.cloned.1.call-start
  8.0 88.8 %all-gather.3.cloned.1.call-done = bf16[2048,2048]{1,0:T(8,128)(2,1)} async-done(((bf16[2048,128]{1,0:T(8,128)(2,1)}), bf16[2048,2048]{1,0:T(8,128)(2,1)}) %all-gather.3.cloned.1.call-update) | async-done | bytes 8388624 | tf_op jit(solution)/shard_map/all_gather | solution.py:51
  96.8 8.6 %fusion.47 = f32[2048,352]{0,1:T(8,128)} fusion(bf16[2048,2048]{1,0:T(8,128)(2,1)} %all-gather.3.cloned.1.call-done, bf16[2048,352]{0,1:T(8,128)(2,1)} %param.13), kind=kOutput, calls=%fused_computation.92 | convolution fusion | flops 2952790016 | bytes 12713984 | tf_op jit(solution)/shard_map/dot_general | solution.py:52
  105.3 13.8 %fusion.1 = f32[2048,2048]{1,0:T(8,128)} fusion(bf16[352,2048]{1,0:T(8,128)(2,1)S(1)} %copy-done, bf16[2048,2048]{1,0:T(8,128)(2,1)} %all-gather.3.cloned.1.call-done, bf16[2048,352]{0,1:T(8,128)(2,1)S(1)} %copy-done.9, f32[2048,352]{0,1:T(8,128)} %fusion.47), kind=kOutput, calls=%fused_computation.4 | convolution fusion | flops 5909905408 | bytes 30932992 | tf_op jit(solution)/shard_map/dot_general | solution.py:55
  119.2 0.0 copy-start.8
  119.2 0.0 reduce-scatter.5.cloned.1.call-update
  119.2 0.0 all-gather.5.cloned.1.call-start
  119.3 0.6 copy-done.11
  119.8 0.6 dynamic-slice
  121.1 0.2 dynamic-update-slice
  121.3 12.2 %all-reduce = s32[1024]{0:T(1024)S(1)} all-reduce(s32[1024]{0:T(1024)S(1)} %dynamic-update-slice), channel_id=1, replica_groups=mesh['dp'=16,'mp'=16] {'dp'}, use_global_device_ids=true, to_apply=%add | all-reduce | flops 1024 | bytes 8192
  133.6 101.4 %reduce-scatter.5.cloned.1.call-done = f32[2048,128]{1,0:T(8,128)} async-done(((f32[2048,2048]{1,0:T(8,128)}), f32[2048,128]{1,0:T(8,128)}) %reduce-scatter.5.cloned.1.call-update) | async-done | bytes 1048592 | tf_op jit(solution)/shard_map/reduce_scatter | solution.py:57
  234.9 1.5 bitcast_reduce_fusion
  236.4 0.0 copy-start.3
  236.4 0.0 copy-start.4
  236.4 19.1 %all_gather.14 = bf16[1024,128]{1,0:T(8,128)(2,1)S(1)} all-gather(bf16[64,128]{1,0:T(8,128)(2,1)S(1)} %multiply_convert_fusion.2), channel_id=1, replica_groups=mesh['dp'=16,'mp'=16] {'dp'}, dimensions={0}, use_global_device_ids=true | all-gather | bytes 278528 | tf_op jit(solution)/shard_map/all_gather | solution.py:62
  255.6 3.1 scatter_custom_fusion
  258.7 0.1 fusion.15
  258.9 31.1 %psum.28 = f32[256]{0:T(256)S(1)} all-reduce(f32[256]{0:T(256)S(1)} %fusion.15), channel_id=1, replica_groups=mesh['dp'=16,'mp'=16] {'mp'}, use_global_device_ids=true, to_apply=%region_4.5 | all-reduce | flops 256 | bytes 2048 | tf_op jit(solution)/shard_map/psum | solution.py:77
  289.9 0.7 fusion.17
  290.7 0.0 all-gather.5.cloned.1.call-update
  290.7 0.2 reduce-scatter.7.cloned.1.call-start
  291.7 0.7 fusion.14
  292.4 0.2 multiply_cosine_fusion
  292.6 1.6 constant_dynamic-slice_fusion
  294.2 44.2 %all-gather.5.cloned.1.call-done = bf16[256,2048]{1,0:T(8,128)(2,1)} async-done(((bf16[256,128]{1,0:T(8,128)(2,1)}), bf16[256,2048]{1,0:T(8,128)(2,1)}) %all-gather.5.cloned.1.call-update) | async-done | bytes 1048592 | tf_op jit(solution)/shard_map/all_gather | solution.py:87
  338.3 1.9 fusion.7
  340.3 0.9 fusion.30
  341.2 1.7 fusion.48
  343.0 1.1 fusion.4
  344.1 0.2 convolution_convert_fusion.2
  344.3 0.5 convolution_convert_fusion
  344.8 1.3 copy.18
  346.1 0.0 reduce-scatter.7.cloned.1.call-update
  346.1 0.0 all-reduce.4.cloned.1.call-start
  346.2 0.2 fusion.5
  346.4 77.1 %reduce-scatter.7.cloned.1.call-done = bf16[128,256]{1,0:T(8,128)(2,1)} async-done(((bf16[2048,256]{1,0:T(8,128)(2,1)}), bf16[128,256]{1,0:T(8,128)(2,1)}) %reduce-scatter.7.cloned.1.call-update) | async-done | bytes 65552
  423.5 0.9 copy.19
  424.5 0.7 multiply_reduce_fusion
  425.2 31.3 %all-reduce.1 = (f32[1024]{0:T(1024)S(1)}, f32[256]{0:T(256)S(1)}) all-reduce(f32[1024]{0:T(1024)S(1)} %fusion.5, f32[256]{0:T(256)S(1)} %get-tuple-element.9), channel_id=1, replica_groups=mesh['dp'=16,'mp'=16] {'mp'}, use_global_device_ids=true, to_apply=%region_10.11 | all-reduce | flops 1280 | bytes 10240 | tf_op jit(solution)/shard_map/psum | solution.py:64
  456.6 1.3 convolution_convert_fusion.1
  457.9 0.0 all-reduce.4.cloned.1.call-update
  457.9 99.4 %all-reduce.4.cloned.1.call-done = bf16[256,1024]{1,0:T(8,128)(2,1)} async-done(((bf16[256,1024]{1,0:T(8,128)(2,1)}), bf16[256,1024]{1,0:T(8,128)(2,1)}) %all-reduce.4.cloned.1.call-update) | async-done | bytes 524304 | tf_op jit(solution)/shard_map/psum | solution.py:117
  557.3 1.4 exponential_reduce_fusion
  558.7 0.6 compare_select_fusion.1
  (31 shorter events, 0.1 us)
Async XLA Ops:
  7.2 98.2 %copy-start = (bf16[352,2048]{1,0:T(8,128)(2,1)S(1)}, bf16[352,2048]{1,0:T(8,128)(2,1)}, u32[]{:S(2)}) copy-start(bf16[352,2048]{1,0:T(8,128)(2,1)} %param.15) | copy-start | bytes 4325380
  7.2 89.6 %all-gather.3.cloned.1.call-start = ((), (), s32[]{:S(2)}) async-start(), calls=%async_computation.2 | async-start | bytes 8912896 | tf_op jit(solution)/shard_map/all_gather | solution.py:51
  7.9 97.4 %copy-start.9 = (bf16[2048,352]{0,1:T(8,128)(2,1)S(1)}, bf16[2048,352]{0,1:T(8,128)(2,1)}, u32[]{:S(2)}) copy-start(bf16[2048,352]{0,1:T(8,128)(2,1)} %param.14) | copy-start | bytes 4325380
  7.9 227.0 %reduce-scatter.5.cloned.1.call-start = ((), (), s32[]{:S(2)}) async-start(), calls=%async_computation.3 | async-start | bytes 17825792 | tf_op jit(solution)/shard_map/reduce_scatter | solution.py:57
  119.1 0.7 copy-start.11
  119.2 1.9 copy-start.10
  119.2 115.8 %copy-start.1 = (bf16[2048,128]{1,0:T(8,128)(2,1)S(1)}, bf16[2048,128]{1,0:T(8,128)(2,1)}, u32[]{:S(2)}) copy-start(bf16[2048,128]{1,0:T(8,128)(2,1)} %param.12) | copy-start | bytes 1572868
  119.2 170.8 %copy-start.8 = (f32[128]{0:T(128)S(1)}, f32[128]{0:T(128)}, u32[]{:S(2)}) copy-start(f32[128]{0:T(128)} %param.16) | copy-start | bytes 1540
  119.2 219.1 %all-gather.5.cloned.1.call-start = ((), (), s32[]{:S(2)}) async-start(), calls=%async_computation.4 | async-start | bytes 1114112 | tf_op jit(solution)/shard_map/all_gather | solution.py:87
  236.4 104.8 %copy-start.3 = (bf16[2048,128]{1,0:T(8,128)(2,1)S(1)}, bf16[2048,128]{1,0:T(8,128)(2,1)}, u32[]{:S(2)}) copy-start(bf16[2048,128]{1,0:T(8,128)(2,1)} %param.17) | copy-start | bytes 1572868
  236.4 106.5 %copy-start.4 = (bf16[64,128]{1,0:T(8,128)(2,1)}, bf16[64,128]{1,0:T(8,128)(2,1)S(1)}, u32[]{:S(2)}) copy-start(bf16[64,128]{1,0:T(8,128)(2,1)S(1)} %multiply_convert_fusion.2) | copy-start | bytes 49156
  290.7 132.8 %reduce-scatter.7.cloned.1.call-start = ((), (), s32[]{:S(2)}) async-start(), calls=%async_computation.6 | async-start | bytes 1114112
  291.6 46.7 %copy-start.7 = (f32[32]{0:T(128)}, f32[32]{0:T(128)S(1)}, u32[]{:S(2)}) copy-start(f32[32]{0:T(128)S(1)} %negate_power_fusion) | copy-start | bytes 388
  291.6 46.7 %copy-start.5 = (f32[256]{0:T(256)}, f32[256]{0:T(256)S(1)}, u32[]{:S(2)}) copy-start(f32[256]{0:T(256)S(1)} %iota_convert_fusion) | copy-start | bytes 3076
  340.2 4.1 copy-start.2
  344.8 212.5 %copy-start.6 = (s32[256]{0:T(256)S(1)}, s32[256]{0:T(256)}, u32[]{:S(2)}) copy-start(s32[256]{0:T(256)} %param.23) | copy-start | bytes 3076
  346.1 211.1 %all-reduce.4.cloned.1.call-start = ((), (), s32[]{:S(2)}) async-start(), calls=%async_computation.5 | async-start | bytes 1048576 | tf_op jit(solution)/shard_map/psum | solution.py:117
Sparse Core Ops, SparseCore 0:
  10.4 86.2 all-gather.2
  119.3 115.5 reduce-scatter.4
  290.8 47.4 all-gather.4
  346.3 77.1 reduce-scatter.6
  458.0 99.1 all-reduce.3
where the time goes:
time: 566 us
  waiting for transfers between devices  412 us (73%)
  blocking collectives  93.8 us (17%)
  matrix products  29.1 us (5%)
  between operations  15.4 us (3%)
  local copies, waits for them, and re-layouts  8.46 us (1%)
  other arithmetic  7.2 us (1%)
    reduce_scatter x1, waiting for transfers between devices, local(): lax.psum_scatter(mixed_rows, 'mp', scatter_dimension=1, tiled=True)  101 us
    psum x1, waiting for transfers between devices, local(): lax.psum(partial_logits.astype(jnp.bfloat16), 'mp').astype(jnp.float32)  99.4 us
    all_gather x1, waiting for transfers between devices, local(): shard_piece = lax.all_gather(item_tokens, 'mp', axis=1, tiled=True)  88.8 us
    unnamed x6, waiting for transfers between devices  77.8 us
    all_gather x1, waiting for transfers between devices, local(): shard_piece = lax.all_gather(normed, 'mp', axis=1, tiled=True)  44.2 us
    psum x1, blocking collectives, local(): item_square = lax.psum(jnp.sum(all_wide * all_wide, axis=-1), 'mp')  31.3 us
    psum x1, blocking collectives, local(): square_sum = lax.psum(jnp.sum(states_wide * states_wide, axis=-1), 'mp')  31.1 us
    all_gather x1, blocking collectives, local(): all_items = lax.all_gather(item_embeddings, 'dp', axis=0, tiled=True)  19.1 us
  transfers between devices with their start and end apart: 5, of which 5 were waited for; matrix products, arithmetic and copies ran while one was open for 1% of the time, Pallas kernels for 0%

commit v1 on v0

v1 whole, which is shorter than its diff:
```python
import functools

import jax
import jax.numpy as jnp
import numpy as np
from jax import lax
from jax.experimental import pallas as pl
from jax.experimental.pallas import tpu as pltpu
from jax.sharding import PartitionSpec as P

HEAD_DIM = 64
ITEM_TOK = 32
SCALE = 20.0
SHORT = 32
LANES = 128
RING = 4
CHUNKS = 8
MESH = pl.DeviceIdType.MESH
BF16 = jnp.bfloat16
F32 = jnp.float32
NT = (((1,), (1,)), ((), ()))


def rope_tables(positions):
    half = HEAD_DIM // 2
    exponent = np.arange(half, dtype=np.float32) * np.float32(2.0 / HEAD_DIM)
    frequency = (10000.0 ** (-exponent.astype(np.float64))).astype(np.float32)
    angles = np.arange(positions, dtype=np.float32)[:, None] * frequency[None, :]
    angles = angles.astype(np.float64)
    cosine, sine = np.cos(angles), np.sin(angles)
    cos_table = np.concatenate([cosine, cosine, cosine, cosine], axis=1)
    sin_table = np.concatenate([-sine, sine, -sine, sine], axis=1)
    return cos_table.astype(np.float32), sin_table.astype(np.float32)


def kernel(
    sizes,
    tok, wg, wu, wd, wq, wk, wv, wo, gain, slot, cos_t, sin_t,
    emb_out, us_out, loss_out,
    g_buf, wg_v, wu_v, wd_v, wq_v, wk_v, wv_v, wo_v,
    pooled, tok_mean, s1, r1, items, x_buf, it_buf, iu, kv_long, s5, r5, us_long, u_buf,
    gains, slots, tp, ll,
    w_sem, g_send, g_recv, mp_send, mp_recv, r1_recv, it_sem, dp_send, dp_recv, item_recv, gs_sem,
):
    n_dp, n_mp, rows, ff, item_dev, short, positions = sizes
    n_items = n_dp * item_dev
    long_rows = positions // n_dp
    mine = short + long_rows
    chunk_items = n_items // n_mp
    chunk_rows = rows // CHUNKS
    pool_items = chunk_rows // ITEM_TOK
    halves = 2
    half_items = item_dev // halves
    half_chunks = CHUNKS // halves
    d = lax.axis_index("dp")
    m = lax.axis_index("mp")
    sibling = d + 1 - 2 * lax.rem(d, 2)

    def to_mp(src, dst, send_sem, recv_sem, j):
        return pltpu.make_async_remote_copy(
            src_ref=src, dst_ref=dst, send_sem=send_sem, recv_sem=recv_sem,
            device_id={"mp": j}, device_id_type=MESH,
        )

    def to_dp(src, dst, send_sem, recv_sem, j):
        return pltpu.make_async_remote_copy(
            src_ref=src, dst_ref=dst, send_sem=send_sem, recv_sem=recv_sem,
            device_id={"dp": j}, device_id_type=MESH,
        )

    def wait_for(ref, sem):
        pltpu.make_async_copy(ref, ref, sem).wait()

    barrier = pltpu.get_barrier_semaphore()
    for k in range(1, n_mp):
        pl.semaphore_signal(
            barrier, inc=1, device_id={"mp": lax.rem(m + k, n_mp)}, device_id_type=MESH
        )
    for k in range(1, n_dp):
        pl.semaphore_signal(
            barrier, inc=1, device_id={"dp": lax.rem(d + k, n_dp)}, device_id_type=MESH
        )

    kv_block = pl.ds(pl.multiple_of((m // 8) * LANES, LANES), LANES)
    loads = [
        (tok, g_buf.at[m]), (wg, wg_v), (wu, wu_v), (wd, wd_v), (wq, wq_v),
        (wk.at[:, kv_block], wk_v), (wv.at[:, kv_block], wv_v), (wo, wo_v),
    ]
    copies = [pltpu.make_async_copy(a, b, w_sem.at[i]) for i, (a, b) in enumerate(loads)]
    for copy in copies:
        copy.start()
    gains[m] = gain[...]
    slots[d] = jnp.concatenate(
        [slot[...], jnp.full((1, LANES - item_dev), -1, jnp.int32)], axis=1
    )
    pl.semaphore_wait(barrier, n_mp + n_dp - 2)

    x_at, y_at = m // RING, lax.rem(m, RING)

    def place(c, o1, o2):
        p = lax.rem(c, 2)
        c1 = x_at * (1 - p) + y_at * p
        c2 = y_at * (1 - p) + x_at * p
        return lax.rem(c1 + o1, RING) * (RING - 3 * p) + lax.rem(c2 + o2, RING) * (1 + 3 * p)

    def chunk(c):
        return pl.ds(pl.multiple_of(c * chunk_rows, chunk_rows), chunk_rows)

    def forward(c, block, target, group):
        to_mp(
            g_buf.at[block, chunk(c)], g_buf.at[block, chunk(c)],
            g_send.at[c], g_recv.at[c, group], target,
        ).start()

    def own(c, target, group):
        to_mp(
            tok.at[chunk(c)], g_buf.at[m, chunk(c)], g_send.at[c], g_recv.at[c, group], target
        ).start()

    def arrived(c, group, count):
        wait_for(g_buf.at[pl.ds(0, count), chunk(c)], g_recv.at[c, group])

    def stage_own(c):
        for o in (1, 3):
            own(c, place(c, o, 0), 0)
        for o in (1, 3):
            own(c, place(c, 0, o), 2)

    def stage_first(c):
        arrived(c, 0, 2)
        way = lax.rem(c // 2, 2)
        forward(c, place(c, 3 - 2 * way, 0), place(c, 1 + 2 * way, 0), 1)
        for o1 in (1, 3):
            for o2 in (1, 3):
                forward(c, place(c, o1, 0), place(c, 0, o2), 2)

    def stage_opposite(c):
        arrived(c, 1, 1)
        for o2 in (1, 3):
            forward(c, place(c, 2, 0), place(c, 0, o2), 2)

    def stage_second(c):
        arrived(c, 2, 8)
        for o1 in (0, 2):
            forward(c, place(c, o1, 3), place(c, 0, 1), 3)
        for o1 in (1, 3):
            forward(c, place(c, o1, 1), place(c, 0, 3), 3)

    pool_of = lax.broadcasted_iota(jnp.int32, (pool_items, chunk_rows), 1) // ITEM_TOK
    pool_row = lax.broadcasted_iota(jnp.int32, (pool_items, chunk_rows), 0)
    pool = (pool_of == pool_row).astype(F32).astype(BF16)

    def stage_compute(c):
        arrived(c, 3, 4)
        here = chunk(c)
        wide = jnp.concatenate([g_buf[k, here, :] for k in range(n_mp)], axis=1)
        gate = jnp.dot(wide, wg_v[...], preferred_element_type=F32)
        up = jnp.dot(wide, wu_v[...], preferred_element_type=F32)
        hidden = (gate / (1.0 + jnp.exp(-gate)) * up).astype(BF16)
        out_rows = pl.ds(pl.multiple_of(c * pool_items, pool_items), pool_items)
        pooled[out_rows, :] = jnp.dot(pool, hidden, preferred_element_type=F32)
        tok_mean[out_rows, :] = jnp.dot(pool, g_buf[m, here, :], preferred_element_type=F32)

    def stage_down(h):
        here = pl.ds(pl.multiple_of(h * half_items, half_items), half_items)
        mean = (pooled[here, :] * (1.0 / ITEM_TOK)).astype(BF16)
        part = jnp.dot(mean, wd_v[...], preferred_element_type=F32).astype(BF16)
        for j in range(n_mp):
            s1[j, here, :] = part[:, j * LANES : (j + 1) * LANES]
        r1[m, here, :] = s1[m, here, :]
        for k in range(1, n_mp):
            j = lax.rem(m + k, n_mp)
            to_mp(s1.at[j, here], r1.at[m, here], mp_send.at[0], r1_recv.at[h], j).start()

    def step(i, carry):
        @pl.when(i < CHUNKS)
        def _():
            stage_own(i)

        @pl.when((i >= 1) & (i < CHUNKS + 1))
        def _():
            stage_first(i - 1)

        @pl.when((i >= 2) & (i < CHUNKS + 2))
        def _():
            stage_opposite(i - 2)

        @pl.when((i >= 3) & (i < CHUNKS + 3))
        def _():
            stage_second(i - 3)

        @pl.when(i == 4)
        def _():
            for copy in copies:
                copy.wait()

        @pl.when(i >= 4)
        def _():
            c = i - 4
            stage_compute(c)

            @pl.when(lax.rem(c, half_chunks) == half_chunks - 1)
            def _():
                stage_down(c // half_chunks)

        return carry

    for k in range(1, n_mp):
        j = lax.rem(m + k, n_mp)
        to_mp(gains.at[m], gains.at[m], gs_sem.at[0], gs_sem.at[1], j).start()
    for k in range(1, n_dp):
        j = lax.rem(d + k, n_dp)
        to_dp(slots.at[d], slots.at[d], gs_sem.at[2], gs_sem.at[3], j).start()

    lax.fori_loop(0, CHUNKS + 4, step, 0)

    for i, (ref, count) in enumerate(((gains, n_mp), (gains, n_mp), (slots, n_dp), (slots, n_dp))):
        wait_for(ref.at[pl.ds(0, count - 1)], gs_sem.at[i])

    slot_row = jnp.concatenate([slots[k][:, :item_dev] for k in range(n_dp)], axis=1)
    last = (slot_row >= 0) & (jnp.bitwise_and(slot_row, positions - 1) == positions - 1)
    long_base = jnp.max(
        jnp.where(last, slot_row, positions - 1), axis=1, keepdims=True
    ) - (positions - 1)
    is_long = long_base == d * positions
    row = lax.broadcasted_iota(jnp.int32, (LANES, 1), 0)
    position = jnp.where(row < short, row, row - short + d * long_rows)
    row_slot = jnp.where(row < short, d * positions, long_base) + position
    row_slot = jnp.where(row < mine, row_slot, -2)
    holds = jnp.where(slot_row == row_slot[:mine], 1.0, 0.0).astype(BF16)
    next_slot = jnp.where((position + 1 < positions) & (row < mine), row_slot + 1, -2)
    follows = jnp.where(slot_row == next_slot, 1.0, 0.0).astype(BF16)
    valid = jnp.sum(holds.astype(F32), axis=1, keepdims=True)
    has_target = lax.dot_general(
        jnp.ones((8, n_items), BF16), follows, NT, preferred_element_type=F32
    )
    item_id = lax.broadcasted_iota(jnp.int32, (n_items, chunk_items), 0)
    chunk_id = lax.broadcasted_iota(jnp.int32, (n_items, chunk_items), 1) + m * chunk_items
    to_chunk = jnp.where(item_id == chunk_id, 1.0, 0.0).astype(BF16)
    picks = jnp.dot(follows[:mine], to_chunk, preferred_element_type=F32)

    for h in range(halves):
        wait_for(r1.at[pl.ds(0, n_mp - 1), pl.ds(h * half_items, half_items)], r1_recv.at[h])
    total = tok_mean[...] * (1.0 / ITEM_TOK)
    for j in range(n_mp):
        total = total + r1[j].astype(F32)
    embedding = total.astype(BF16)
    emb_out[...] = embedding

    def dp_block(k):
        return pl.ds(pl.multiple_of(k * item_dev, item_dev), item_dev)

    items[dp_block(d), :] = embedding
    for k in range(n_dp // 2):
        j = lax.rem(d + 2 * k, n_dp) if k else sibling
        to_dp(
            items.at[dp_block(d)], items.at[dp_block(d)], dp_send.at[0], item_recv.at[d], j
        ).start()
    for k in range(1, n_dp // 2):
        j = lax.rem(d + n_dp - 2 * k, n_dp)
        wait_for(items.at[dp_block(j)], item_recv.at[j])
        to_dp(
            items.at[dp_block(j)], items.at[dp_block(j)], dp_send.at[0], item_recv.at[j], sibling
        ).start()
    for k in range(n_dp // 2):
        j = lax.rem(sibling + n_dp - 2 * k, n_dp)
        wait_for(items.at[dp_block(j)], item_recv.at[j])

    placed = jnp.dot(holds, items[...], preferred_element_type=F32)
    x_buf[m] = placed.astype(BF16)
    for k in range(1, n_mp):
        j = lax.rem(m + k, n_mp)
        to_mp(x_buf.at[m], x_buf.at[m], mp_send.at[1], mp_recv.at[1], j).start()

    def item_block(k):
        return pl.ds(pl.multiple_of(k * chunk_items, chunk_items), chunk_items)

    it_buf[m] = items[item_block(m), :]
    for k in range(1, n_mp):
        j = lax.rem(m + k, n_mp)
        to_mp(items.at[item_block(j)], it_buf.at[m], it_sem.at[0], it_sem.at[1], j).start()
    wait_for(x_buf.at[pl.ds(0, n_mp - 1)], mp_recv.at[1])

    states = [x_buf[j].astype(F32) for j in range(n_mp)]
    squares = states[0] * states[0]
    for block in states[1:]:
        squares = squares + block * block
    features = n_mp * LANES
    inverse = lax.rsqrt(jnp.sum(squares, axis=1, keepdims=True) / features + 1e-05)
    normed = jnp.concatenate(
        [(states[j] * inverse * gains[j]).astype(BF16) for j in range(n_mp)], axis=1
    )
    query = jnp.dot(normed, wq_v[...], preferred_element_type=F32)
    key = jnp.dot(normed, wk_v[...], preferred_element_type=F32)
    value = jnp.dot(normed, wv_v[...], preferred_element_type=F32)

    long_here = pl.ds(pl.multiple_of(d * long_rows, long_rows), long_rows)
    cosine = jnp.concatenate([cos_t[0:short, :], cos_t[long_here, :]], axis=0)
    sine = jnp.concatenate([sin_t[0:short, :], sin_t[long_here, :]], axis=0)
    lane = lax.broadcasted_iota(jnp.int32, (mine, LANES), 1)
    low = lax.rem(lane, HEAD_DIM) < HEAD_DIM // 2
    left = lane < HEAD_DIM

    def rotate(v):
        swapped = jnp.where(
            low,
            pltpu.roll(v, LANES - HEAD_DIM // 2, axis=1),
            pltpu.roll(v, HEAD_DIM // 2, axis=1),
        )
        return v * cosine + swapped * sine

    query = rotate(query) * HEAD_DIM ** (-0.5)
    key = rotate(key)
    first_kv = (lane * 0 + lax.rem(m // 4, 2)) == 0
    key_part = jnp.where(first_kv, key, pltpu.roll(key, HEAD_DIM, axis=1))
    value_part = jnp.where(first_kv, pltpu.roll(value, HEAD_DIM, axis=1), value)
    pair = jnp.where(left, key_part, value_part).astype(BF16)
    kv_long[long_here, :] = pair[short:]
    for k in range(1, n_dp):
        j = lax.rem(d + k, n_dp)
        to_dp(
            kv_long.at[long_here], kv_long.at[long_here], dp_send.at[1], dp_recv.at[1], j
        ).start()

    head0 = jnp.where(left, query, 0.0).astype(BF16)
    head1 = jnp.where(left, pltpu.roll(query, HEAD_DIM, axis=1), 0.0).astype(BF16)

    def attend(q_rows, keys, first_position):
        count, n_keys = q_rows.shape[0], keys.shape[0]
        scores = lax.dot_general(q_rows, keys, NT, preferred_element_type=F32)
        at = lax.rem(lax.broadcasted_iota(jnp.int32, (count, n_keys), 0), count // 2)
        of = lax.broadcasted_iota(jnp.int32, (count, n_keys), 1)
        weights = jnp.where(of <= at + first_position, jnp.exp(scores), 0.0)
        weights = (weights / jnp.sum(weights, axis=1, keepdims=True)).astype(BF16)
        mixed = jnp.dot(weights, keys, preferred_element_type=F32)
        top, bottom = mixed[: count // 2], mixed[count // 2 :]
        at_left = lax.broadcasted_iota(jnp.int32, top.shape, 1) < HEAD_DIM
        return jnp.where(at_left, pltpu.roll(top, HEAD_DIM, axis=1), bottom).astype(BF16)

    short_rows = attend(
        jnp.concatenate([head0[:short], head1[:short]], axis=0), pair[:short], 0
    )
    wait_for(
        kv_long.at[pl.ds(0, (n_dp - 1) * long_rows)], dp_recv.at[1]
    )
    rest = attend(
        jnp.concatenate([head0[short:], head1[short:]], axis=0), kv_long[...], d * long_rows
    )
    attended = jnp.concatenate([short_rows, rest], axis=0)
    attn = jnp.dot(attended, wo_v[...], preferred_element_type=F32).astype(BF16)
    for j in range(n_mp):
        s5[j] = attn[:, j * LANES : (j + 1) * LANES]
    r5[m] = s5[m]
    for k in range(1, n_mp):
        j = lax.rem(m + k, n_mp)
        to_mp(s5.at[j], r5.at[m], mp_send.at[2], mp_recv.at[2], j).start()

    wait_for(it_buf.at[pl.ds(0, n_mp - 1)], it_sem.at[1])
    wide_items = [it_buf[j].astype(F32) for j in range(n_mp)]
    item_squares = wide_items[0] * wide_items[0]
    for block in wide_items[1:]:
        item_squares = item_squares + block * block
    item_scale = lax.rsqrt(jnp.sum(item_squares, axis=1, keepdims=True) + 1e-06)
    for j in range(n_mp):
        iu[:, j * LANES : (j + 1) * LANES] = (wide_items[j] * item_scale).astype(BF16)

    wait_for(r5.at[pl.ds(0, n_mp - 1)], mp_recv.at[2])
    combined = placed
    for j in range(n_mp):
        combined = combined + r5[j].astype(F32)
    combined = jnp.where(valid > 0.5, combined, 0.0).astype(BF16)
    u_buf[m] = combined
    for k in range(1, n_mp):
        j = lax.rem(m + k, n_mp)
        to_mp(u_buf.at[m], u_buf.at[m], mp_send.at[3], mp_recv.at[3], j).start()
    us_long[long_here, :] = combined[short:]
    for k in range(1, n_dp):
        j = lax.rem(d + k, n_dp)
        to_dp(
            us_long.at[long_here], us_long.at[long_here], dp_send.at[2], dp_recv.at[2], j
        ).start()

    wait_for(u_buf.at[pl.ds(0, n_mp - 1)], mp_recv.at[3])
    users = [u_buf[j] for j in range(n_mp)]
    user_squares = users[0].astype(F32) * users[0].astype(F32)
    for block in users[1:]:
        user_squares = user_squares + block.astype(F32) * block.astype(F32)
    user_scale = lax.rsqrt(jnp.sum(user_squares, axis=1, keepdims=True) + 1e-06)
    logits = lax.dot_general(
        jnp.concatenate(users, axis=1), iu[...], NT, preferred_element_type=F32
    ) * (SCALE * user_scale)
    stack = jnp.concatenate(
        [jnp.exp(logits), logits * picks, jnp.zeros((LANES - 2 * mine, chunk_items), F32)], axis=0
    )
    sums = lax.dot_general(
        jnp.ones((8, chunk_items), F32), stack, NT,
        precision=lax.Precision.HIGHEST, preferred_element_type=F32,
    )
    tp[m] = sums[0:1]
    for k in range(1, n_mp):
        j = lax.rem(m + k, n_mp)
        to_mp(tp.at[m], tp.at[m], mp_send.at[4], mp_recv.at[4], j).start()

    wait_for(us_long.at[pl.ds(0, (n_dp - 1) * long_rows)], dp_recv.at[2])
    short_states = jnp.concatenate(
        [combined[:short].astype(F32), jnp.zeros((positions - short, LANES), F32)], axis=0
    )
    us_out[...] = jnp.where(is_long, us_long[...].astype(F32), short_states).astype(BF16)

    wait_for(tp.at[pl.ds(0, n_mp - 1)], mp_recv.at[4])
    sums = tp[0]
    for j in range(1, n_mp):
        sums = sums + tp[j]
    sums = jnp.broadcast_to(sums, (8, LANES))
    counted = has_target > 0.5
    picked = pltpu.roll(sums, LANES - mine, axis=1)
    loss = jnp.where(counted, jnp.log(jnp.where(counted, sums, 1.0)) - picked, 0.0)
    at_lane = lax.broadcasted_iota(jnp.int32, (LANES, positions), 0)
    at_position = lax.broadcasted_iota(jnp.int32, (LANES, positions), 1)
    chosen = (at_lane >= short) & (at_lane < mine)
    chosen = chosen & (at_position == at_lane - short + d * long_rows)
    spread = jnp.dot(
        loss, jnp.where(chosen, 1.0, 0.0),
        precision=lax.Precision.HIGHEST, preferred_element_type=F32,
    )
    ll[d] = spread[0:1]
    for k in range(1, n_dp):
        j = lax.rem(d + k, n_dp)
        to_dp(ll.at[d], ll.at[d], dp_send.at[3], dp_recv.at[3], j).start()
    same = (at_lane < short) & (at_position == at_lane)
    short_loss = jnp.dot(
        loss, jnp.where(same, 1.0, 0.0),
        precision=lax.Precision.HIGHEST, preferred_element_type=F32,
    )[0:1]
    wait_for(ll.at[pl.ds(0, n_dp - 1)], dp_recv.at[3])
    long_loss = ll[0]
    for j in range(1, n_dp):
        long_loss = long_loss + ll[j]
    loss_out[...] = jnp.where(is_long, long_loss, short_loss)

    for c in range(CHUNKS):
        wait_for(g_buf.at[pl.ds(0, n_mp - 1), pl.ds(c * chunk_rows, chunk_rows)], g_send.at[c])
    wait_for(s1.at[pl.ds(0, n_mp - 1)], mp_send.at[0])
    wait_for(x_buf.at[pl.ds(0, n_mp - 1)], mp_send.at[1])
    wait_for(s5.at[pl.ds(0, n_mp - 1)], mp_send.at[2])
    wait_for(u_buf.at[pl.ds(0, n_mp - 1)], mp_send.at[3])
    wait_for(tp.at[pl.ds(0, n_mp - 1)], mp_send.at[4])
    wait_for(it_buf.at[pl.ds(0, n_mp - 1)], it_sem.at[0])
    wait_for(items.at[pl.ds(0, (n_dp - 1) * item_dev)], dp_send.at[0])
    wait_for(kv_long.at[pl.ds(0, (n_dp - 1) * long_rows)], dp_send.at[1])
    wait_for(us_long.at[pl.ds(0, (n_dp - 1) * long_rows)], dp_send.at[2])
    wait_for(ll.at[pl.ds(0, n_dp - 1)], dp_send.at[3])


def solution(mesh, short=SHORT):
    n_dp, n_mp = mesh.shape["dp"], mesh.shape["mp"]

    def local(tok, wg, wu, wd, gain, wq, wk, wv, wo, item_slot, lengths, targets):
        rows, features = tok.shape[0], wg.shape[0]
        ff, item_dev, positions = wg.shape[1], item_slot.shape[0], targets.shape[0]
        n_items = n_dp * item_dev
        mine = short + positions // n_dp
        cos_table, sin_table = rope_tables(positions)
        any_spec = pl.BlockSpec(memory_space=pl.ANY)
        vmem = pl.BlockSpec(memory_space=pltpu.VMEM)
        dma = pltpu.SemaphoreType.DMA
        sizes = (n_dp, n_mp, rows, ff, item_dev, short, positions)
        embeddings, states, losses = pl.pallas_call(
            functools.partial(kernel, sizes),
            out_shape=(
                jax.ShapeDtypeStruct((item_dev, LANES), BF16),
                jax.ShapeDtypeStruct((positions, LANES), BF16),
                jax.ShapeDtypeStruct((1, positions), F32),
            ),
            in_specs=[any_spec] * 8 + [vmem] * 4,
            out_specs=(vmem, vmem, vmem),
            scratch_shapes=[
                pltpu.VMEM((n_mp, rows, LANES), BF16),
                pltpu.VMEM((features, ff), BF16),
                pltpu.VMEM((features, ff), BF16),
                pltpu.VMEM((ff, features), BF16),
                pltpu.VMEM((features, LANES), BF16),
                pltpu.VMEM((features, LANES), BF16),
                pltpu.VMEM((features, LANES), BF16),
                pltpu.VMEM((LANES, features), BF16),
                pltpu.VMEM((item_dev, ff), F32),
                pltpu.VMEM((item_dev, LANES), F32),
                pltpu.VMEM((n_mp, item_dev, LANES), BF16),
                pltpu.VMEM((n_mp, item_dev, LANES), BF16),
                pltpu.VMEM((n_items, LANES), BF16),
                pltpu.VMEM((n_mp, mine, LANES), BF16),
                pltpu.VMEM((n_mp, n_items // n_mp, LANES), BF16),
                pltpu.VMEM((n_items // n_mp, features), BF16),
                pltpu.VMEM((positions, LANES), BF16),
                pltpu.VMEM((n_mp, mine, LANES), BF16),
                pltpu.VMEM((n_mp, mine, LANES), BF16),
                pltpu.VMEM((positions, LANES), BF16),
                pltpu.VMEM((n_mp, mine, LANES), BF16),
                pltpu.VMEM((n_mp, 1, LANES), F32),
                pltpu.VMEM((n_dp, 1, LANES), jnp.int32),
                pltpu.VMEM((n_mp, 1, LANES), F32),
                pltpu.VMEM((n_dp, 1, positions), F32),
                dma((8,)),
                dma((CHUNKS,)),
                dma((CHUNKS, 4)),
                dma((5,)),
                dma((5,)),
                dma((2,)),
                dma((2,)),
                dma((4,)),
                dma((4,)),
                dma((n_dp,)),
                dma((4,)),
            ],
            compiler_params=pltpu.CompilerParams(
                collective_id=0, has_side_effects=True, vmem_limit_bytes=48 * 1024 * 1024
            ),
        )(
            tok, wg, wu, wd, wq, wk, wv, wo,
            gain.reshape(1, LANES), item_slot.reshape(1, item_dev),
            jnp.asarray(cos_table), jnp.asarray(sin_table),
        )
        return embeddings, states, losses.reshape(positions)

    return jax.shard_map(
        local,
        mesh=mesh,
        in_specs=(
            P("dp", "mp"), P(None, "mp"), P(None, "mp"), P("mp", None), P("mp"),
            P(None, "mp"), P(), P(), P("mp", None), P("dp"), P("dp"), P("dp"),
        ),
        out_specs=(P("dp", "mp"), P("dp", "mp"), P("dp")),
        check_vma=False,
    )
```

time: 566 us -> 124 us (0.22)
  waiting for transfers between devices: 412 us -> 0 us
  Pallas kernels: 0 us -> 111 us
  blocking collectives: 93.8 us -> 0 us
  matrix products: 29.1 us -> 0 us
  between operations: 15.4 us -> 0.69 us
  other arithmetic: 7.2 us -> 0 us
    all_gather x2 -> x0, waiting for transfers between devices: 133 us -> none  [the longest x1 88.8 us: local(): shard_piece = lax.all_gather(item_tokens, 'mp', axis=1, tiled=True)]
    pallas_call x0 -> x1, Pallas kernels: none -> 111 us  [local(): pl.pallas_call(functools.partial(kernel, sizes), out_shape=(jax.ShapeDtyp...]
    reduce_scatter x1 -> x0, waiting for transfers between devices: 101 us -> none  [local(): lax.psum_scatter(mixed_rows, 'mp', scatter_dimension=1, tiled=True)]
    psum x1 -> x0, waiting for transfers between devices: 99.4 us -> none  [local(): lax.psum(partial_logits.astype(jnp.bfloat16), 'mp').astype(jnp.float32)]
    unnamed x6 -> x0, waiting for transfers between devices: 77.8 us -> none
    psum x2 -> x0, blocking collectives: 62.4 us -> none  [the longest x1 31.3 us: local(): item_square = lax.psum(jnp.sum(all_wide * all_wide, axis=-1), 'mp')]
    dot_general x8 -> x0, matrix products: 29.1 us -> none  [the longest x1 13.8 us: local(): jnp.dot(hidden, down_weight, preferred_element_type=jnp.float32)]
    all_gather x1 -> x0, blocking collectives: 19.1 us -> none  [local(): all_items = lax.all_gather(item_embeddings, 'dp', axis=0, tiled=True)]
  transfers between devices with their start and end apart: 5 -> 0, of which waited for: 5 -> 0; matrix products, arithmetic and copies ran while one was open for 1% -> 0% of each run, Pallas kernels for 0% -> 0%
where the time goes in v1:
time: 124 us
  Pallas kernels  111 us (90%)
  local copies, waits for them, and re-layouts  12.2 us (10%)
    pallas_call x1, Pallas kernels, local(): pl.pallas_call(functools.partial(kernel, sizes), out_shape=(jax.ShapeDtyp...  111 us
    unnamed x25, local copies, waits for them, and re-layouts  12.2 us

profile of v1, /device:TPU:1, one launch (start us, length us, event | category | flops | bytes accessed | tf_op | source)
XLA Modules:
  0.0 123.8 jit_solution(12216069014317013340)
XLA Ops:
  0.6 0.0 copy-start.2
  0.6 2.7 %copy.15.wg = bf16[2048,352]{1,0:T(8,128)(2,1)} copy(bf16[2048,352]{0,1:T(8,128)(2,1)} %param.15) | data formatting | bytes 2883584 | tf_op args[1]
  3.3 0.0 copy-start
  3.3 0.0 copy-start.1
  3.3 0.0 copy-start.8
  3.3 0.0 copy-start.9
  3.3 2.7 %copy.16.wu = bf16[2048,352]{1,0:T(8,128)(2,1)} copy(bf16[2048,352]{0,1:T(8,128)(2,1)} %param.16) | data formatting | bytes 2883584 | tf_op args[2]
  6.1 0.0 copy-done.2
  6.1 0.0 copy-done
  6.1 0.0 copy-done.1
  6.1 0.0 copy-done.8
  6.1 0.0 copy-done.9
  6.1 0.0 copy-start.3
  6.1 1.0 copy-done.3
  7.1 0.0 copy-start.4
  7.1 1.0 copy-done.4
  8.2 0.0 copy-start.5
  8.2 1.0 copy-done.5
  9.2 0.0 copy-start.6
  9.2 0.9 copy-done.6
  10.1 0.0 copy-start.7
  10.1 0.9 copy-done.7
  11.0 111.0 %shard_map.139 = (bf16[64,128]{1,0:T(8,128)(2,1)S(1)}, bf16[256,128]{1,0:T(8,128)(2,1)S(1)}, f32[1,256]{1,0:T(1,128)S(1)}) custom-call(bf16[2048,128]{1,0:T(8,128)(2,1)S(1)} %copy-done.3, bf16[2048,352]{1,0:T(8,128)(2,1)} %copy.15.wg, bf16[2048,352]{1,0:T(8,128)(2,1)} %copy.16.wu, bf16[352,2048]{1,0:T(8,128)(2,1)S(1)} %copy-done, ...), custom_call_target="tpu_custom_call" | custom-call | tf_op jit(solution)/shard_map/pallas_call | solution.py:468
  122.0 0.6 copy.20
  122.6 0.6 copy.21
  123.3 0.6 copy.22
Async XLA Ops:
  0.6 5.4 %copy-start.2 = (bf16[2048,256]{1,0:T(8,128)(2,1)S(1)}, bf16[2048,256]{1,0:T(8,128)(2,1)}, u32[]{:S(2)}) copy-start(bf16[2048,256]{1,0:T(8,128)(2,1)} %wv.1) | copy-start | bytes 3145732
  3.3 2.7 %copy-start = (bf16[352,2048]{1,0:T(8,128)(2,1)S(1)}, bf16[352,2048]{1,0:T(8,128)(2,1)}, u32[]{:S(2)}) copy-start(bf16[352,2048]{1,0:T(8,128)(2,1)} %wd.1) | copy-start | bytes 4325380
  3.3 2.7 %copy-start.1 = (bf16[2048,256]{1,0:T(8,128)(2,1)S(1)}, bf16[2048,256]{1,0:T(8,128)(2,1)}, u32[]{:S(2)}) copy-start(bf16[2048,256]{1,0:T(8,128)(2,1)} %wk.1) | copy-start | bytes 3145732
  3.3 2.7 %copy-start.8 = (f32[128]{0:T(128)S(1)}, f32[128]{0:T(128)}, u32[]{:S(2)}) copy-start(f32[128]{0:T(128)} %param.18) | copy-start | bytes 1540
  3.3 2.8 %copy-start.9 = (s32[64]{0:T(128)S(1)}, s32[64]{0:T(128)}, u32[]{:S(2)}) copy-start(s32[64]{0:T(128)} %param.23) | copy-start | bytes 772
  6.1 1.0 copy-start.3
  7.1 1.0 copy-start.4
  8.2 1.0 copy-start.5
  9.2 0.9 copy-start.6
  10.1 0.9 copy-start.7

commit v2 on v1

--- a/solution.py
+++ b/solution.py
@@ -14,6 +14,7 @@
 SHORT = 32
 LANES = 128
 RING = 4
+SPOT = (0, 2, 3, 1)
 CHUNKS = 8
 MESH = pl.DeviceIdType.MESH
 BF16 = jnp.bfloat16
@@ -37,21 +38,23 @@
     sizes,
     tok, wg, wu, wd, wq, wk, wv, wo, gain, slot, cos_t, sin_t,
     emb_out, us_out, loss_out,
-    g_buf, wg_v, wu_v, wd_v, wq_v, wk_v, wv_v, wo_v,
-    pooled, tok_mean, s1, r1, items, x_buf, it_buf, iu, kv_long, s5, r5, us_long, u_buf,
+    g_buf, tok_v, w2, wg_v, wu_v, wd_v, wq_v, wk_v, wv_v, wo_v,
+    pooled, pooled2, pooled_out, pooled_in, tok_mean, s1, r1, items, x_buf, it_buf, iu, kv_long, s5, r5, us_long, u_buf,
     gains, slots, tp, ll,
-    w_sem, g_send, g_recv, mp_send, mp_recv, r1_recv, it_sem, dp_send, dp_recv, item_recv, gs_sem,
+    w_sem, e_send, e_recv, gx_send, gy_send, g_recv, w2_send, w2_first, w2_up, w2_down, w2_side, p_sem,
+    mp_send, mp_recv, r1_recv, it_sem, dp_send, dp_recv, item_recv, gs_sem,
 ):
     n_dp, n_mp, rows, ff, item_dev, short, positions = sizes
     n_items = n_dp * item_dev
     long_rows = positions // n_dp
     mine = short + long_rows
     chunk_items = n_items // n_mp
-    chunk_rows = rows // CHUNKS
-    pool_items = chunk_rows // ITEM_TOK
-    halves = 2
-    half_items = item_dev // halves
-    half_chunks = CHUNKS // halves
+    half_rows = rows // 2
+    chunk_rows = half_rows // CHUNKS
+    x_rows = chunk_rows // 2
+    span = 2 * chunk_rows
+    pool_items = span // ITEM_TOK
+    half_items = item_dev // 2
     d = lax.axis_index("dp")
     m = lax.axis_index("mp")
     sibling = d + 1 - 2 * lax.rem(d, 2)
@@ -82,13 +85,18 @@
         )
 
     kv_block = pl.ds(pl.multiple_of((m // 8) * LANES, LANES), LANES)
+    at_half = pl.ds(pl.multiple_of((lax.rem(m, RING) // 2) * half_rows, half_rows), half_rows)
+    at_spot = m // RING * RING + lax.rem((lax.rem(m, RING) + 1) // 2, 2) * 2 + lax.rem(m, RING) // 2
     loads = [
-        (tok, g_buf.at[m]), (wg, wg_v), (wu, wu_v), (wd, wd_v), (wq, wq_v),
-        (wk.at[:, kv_block], wk_v), (wv.at[:, kv_block], wv_v), (wo, wo_v),
+        (tok.at[at_half], g_buf.at[at_spot]), (tok, tok_v), (wg, wg_v), (wu, wu_v), (wd, wd_v),
+        (wq, wq_v), (wk.at[:, kv_block], wk_v), (wv.at[:, kv_block], wv_v), (wo, wo_v),
     ]
     copies = [pltpu.make_async_copy(a, b, w_sem.at[i]) for i, (a, b) in enumerate(loads)]
     for copy in copies:
         copy.start()
+    token_of = lax.broadcasted_iota(jnp.int32, (item_dev, rows), 1) // ITEM_TOK
+    token_row = lax.broadcasted_iota(jnp.int32, (item_dev, rows), 0)
+    token_pool = (token_of == token_row).astype(F32).astype(BF16)
     gains[m] = gain[...]
     slots[d] = jnp.concatenate(
         [slot[...], jnp.full((1, LANES - item_dev), -1, jnp.int32)], axis=1
@@ -96,83 +104,141 @@
     pl.semaphore_wait(barrier, n_mp + n_dp - 2)
 
     x_at, y_at = m // RING, lax.rem(m, RING)
-
-    def place(c, o1, o2):
-        p = lax.rem(c, 2)
-        c1 = x_at * (1 - p) + y_at * p
-        c2 = y_at * (1 - p) + x_at * p
-        return lax.rem(c1 + o1, RING) * (RING - 3 * p) + lax.rem(c2 + o2, RING) * (1 + 3 * p)
+    half = y_at // 2
+    pair_at = lax.rem((y_at + 1) // 2, 2)
+    base = x_at * RING + pair_at * 2
+    partner = x_at * RING + 3 - y_at
+    beside = x_at * RING + y_at + 1 - 2 * lax.rem(y_at, 2)
+    x_next = lax.rem(x_at + 1, RING)
+    x_back = lax.rem(x_at + RING - 1, RING)
+    x_far = lax.rem(x_at + 2, RING)
+    ahead, behind = x_next * RING + y_at, x_back * RING + y_at
+    X1, X2, X3, Y1, Y2, Y3 = range(6)
 
     def chunk(c):
         return pl.ds(pl.multiple_of(c * chunk_rows, chunk_rows), chunk_rows)
 
-    def forward(c, block, target, group):
+    def rows_x(c):
+        return pl.ds(pl.multiple_of(c * chunk_rows, 16), x_rows)
+
+    def rows_y(c):
+        return pl.ds(pl.multiple_of(c * chunk_rows + x_rows, 16), chunk_rows - x_rows)
+
+    def forward(start, count, there, sem, stage, c, target):
+        blocks = g_buf.at[pl.ds(start, count), there]
+        to_mp(blocks, blocks, sem.at[c], g_recv.at[c, stage], target).start()
+
+    def arrived(count, there, stage, c):
+        wait_for(g_buf.at[pl.ds(0, count), there], g_recv.at[c, stage])
+
+    def stage_exchange(c):
+        theirs = (1 - half) * half_rows + c * chunk_rows
         to_mp(
-            g_buf.at[block, chunk(c)], g_buf.at[block, chunk(c)],
-            g_send.at[c], g_recv.at[c, group], target,
+            tok.at[pl.ds(pl.multiple_of(theirs, chunk_rows), chunk_rows)],
+            g_buf.at[base + half, chunk(c)], e_send.at[c], e_recv.at[c], partner,
         ).start()
 
-    def own(c, target, group):
-        to_mp(
-            tok.at[chunk(c)], g_buf.at[m, chunk(c)], g_send.at[c], g_recv.at[c, group], target
-        ).start()
-
-    def arrived(c, group, count):
-        wait_for(g_buf.at[pl.ds(0, count), chunk(c)], g_recv.at[c, group])
-
     def stage_own(c):
-        for o in (1, 3):
-            own(c, place(c, o, 0), 0)
-        for o in (1, 3):
-            own(c, place(c, 0, o), 2)
+        wait_for(g_buf.at[0, chunk(c)], e_recv.at[c])
+        forward(base, 2, rows_x(c), gx_send, X1, c, ahead)
+        forward(base, 2, rows_x(c), gx_send, X1, c, behind)
+        forward(base, 2, rows_y(c), gy_send, Y1, c, beside)
 
     def stage_first(c):
-        arrived(c, 0, 2)
-        way = lax.rem(c // 2, 2)
-        forward(c, place(c, 3 - 2 * way, 0), place(c, 1 + 2 * way, 0), 1)
-        for o1 in (1, 3):
-            for o2 in (1, 3):
-                forward(c, place(c, o1, 0), place(c, 0, o2), 2)
-
-    def stage_opposite(c):
-        arrived(c, 1, 1)
-        for o2 in (1, 3):
-            forward(c, place(c, 2, 0), place(c, 0, o2), 2)
+        arrived(2, rows_y(c), Y1, c)
+        forward(x_at * RING, 4, rows_y(c), gy_send, Y2, c, ahead)
+        forward(x_at * RING, 4, rows_y(c), gy_send, Y2, c, behind)
+        arrived(4, rows_x(c), X1, c)
+        forward(x_back * RING + pair_at * 2, 1, rows_x(c), gx_send, X2, c, ahead)
+        forward(x_next * RING + pair_at * 2 + 1, 1, rows_x(c), gx_send, X2, c, behind)
 
     def stage_second(c):
-        arrived(c, 2, 8)
-        for o1 in (0, 2):
-            forward(c, place(c, o1, 3), place(c, 0, 1), 3)
-        for o1 in (1, 3):
-            forward(c, place(c, o1, 1), place(c, 0, 3), 3)
-
-    pool_of = lax.broadcasted_iota(jnp.int32, (pool_items, chunk_rows), 1) // ITEM_TOK
-    pool_row = lax.broadcasted_iota(jnp.int32, (pool_items, chunk_rows), 0)
+        arrived(2, rows_x(c), X2, c)
+        for k in range(RING):
+            forward(k * RING + pair_at * 2, 2, rows_x(c), gx_send, X3, c, beside)
+        arrived(8, rows_y(c), Y2, c)
+        forward(x_back * RING, 2, rows_y(c), gy_send, Y3, c, ahead)
+        forward(x_next * RING + 2, 2, rows_y(c), gy_send, Y3, c, behind)
+
+    def stage_last(c):
+        arrived(8, rows_x(c), X3, c)
+        arrived(4, rows_y(c), Y3, c)
+
+    core = lax.rem(d, 2)
+
+    def piece(steps):
+        return lax.rem(d + n_dp + 2 * steps, n_dp)
+
+    def pass_on(steps, part, target, sem):
+        k = piece(steps)
+        ref = w2.at[k] if part is None else w2.at[k, part]
+        to_dp(ref, ref, w2_send, sem, target).start()
+
+    def weights_start():
+        lanes = pl.ds(pl.multiple_of(d * LANES, LANES), LANES)
+        for part, ref in enumerate((wg, wu)):
+            to_mp(ref.at[:, lanes], w2.at[d, part], w2_send, w2_first, partner).start()
+
+    def weights_step(k):
+        up, down = piece(1), piece(-1)
+        if k == 0:
+            wait_for(w2.at[0], w2_first)
+            pass_on(0, None, up, w2_up.at[0])
+            pass_on(0, None, down, w2_down.at[0])
+            pass_on(0, None, sibling, w2_side)
+            return
+        wait_for(w2.at[0], w2_up.at[k - 1])
+        wait_for(w2.at[0], w2_down.at[k - 1])
+        last = k == n_dp // 4 - 1
+        pass_on(-k, 0 if last else None, up, w2_up.at[k])
+        pass_on(k, 1 if last else None, down, w2_down.at[k])
+        pass_on(-k, None, sibling, w2_side)
+        pass_on(k, None, sibling, w2_side)
+
+    def weights_end():
+        k = n_dp // 4 - 1
+        wait_for(w2.at[0, 0], w2_up.at[k])
+        wait_for(w2.at[0, 1], w2_down.at[k])
+        pass_on(n_dp // 4, None, sibling, w2_side)
+
+    pool_of = lax.broadcasted_iota(jnp.int32, (pool_items, span), 1) // ITEM_TOK
+    pool_row = lax.broadcasted_iota(jnp.int32, (pool_items, span), 0)
     pool = (pool_of == pool_row).astype(F32).astype(BF16)
 
-    def stage_compute(c):
-        arrived(c, 3, 4)
-        here = chunk(c)
-        wide = jnp.concatenate([g_buf[k, here, :] for k in range(n_mp)], axis=1)
-        gate = jnp.dot(wide, wg_v[...], preferred_element_type=F32)
-        up = jnp.dot(wide, wu_v[...], preferred_element_type=F32)
+    def ffn(k, gate_w, up_w, result):
+        here = pl.ds(pl.multiple_of(k * span, span), span)
+        wide = jnp.concatenate(
+            [g_buf[j // RING * RING + SPOT[j % RING], here, :] for j in range(n_mp)], axis=1
+        )
+        gate = lax.dot_general(gate_w, wide, NT, preferred_element_type=F32)
+        up = lax.dot_general(up_w, wide, NT, preferred_element_type=F32)
         hidden = (gate / (1.0 + jnp.exp(-gate)) * up).astype(BF16)
-        out_rows = pl.ds(pl.multiple_of(c * pool_items, pool_items), pool_items)
-        pooled[out_rows, :] = jnp.dot(pool, hidden, preferred_element_type=F32)
-        tok_mean[out_rows, :] = jnp.dot(pool, g_buf[m, here, :], preferred_element_type=F32)
-
-    def stage_down(h):
+        there = pl.ds(pl.multiple_of(k * pool_items, pool_items), pool_items)
+        result[there, :] = lax.dot_general(pool, hidden, NT, preferred_element_type=F32)
+
+    def ffn_own(k):
+        ffn(k, wg_v[...], wu_v[...], pooled)
+
+    def ffn_partner(k):
+        gate_w = jnp.concatenate([w2[j, 0] for j in range(n_mp)], axis=1)
+        up_w = jnp.concatenate([w2[j, 1] for j in range(n_mp)], axis=1)
+        ffn(k, gate_w, up_w, pooled2)
+
+    def stage_down(h, source, order):
         here = pl.ds(pl.multiple_of(h * half_items, half_items), half_items)
-        mean = (pooled[here, :] * (1.0 / ITEM_TOK)).astype(BF16)
-        part = jnp.dot(mean, wd_v[...], preferred_element_type=F32).astype(BF16)
+        part = jnp.dot(source, wd_v[...], preferred_element_type=F32).astype(BF16)
         for j in range(n_mp):
             s1[j, here, :] = part[:, j * LANES : (j + 1) * LANES]
         r1[m, here, :] = s1[m, here, :]
         for k in range(1, n_mp):
             j = lax.rem(m + k, n_mp)
-            to_mp(s1.at[j, here], r1.at[m, here], mp_send.at[0], r1_recv.at[h], j).start()
+            to_mp(s1.at[j, here], r1.at[m, here], mp_send.at[0], r1_recv.at[order], j).start()
 
     def step(i, carry):
+        @pl.when(i < CHUNKS - 2)
+        def _():
+            stage_exchange(i + 2)
+
         @pl.when(i < CHUNKS)
         def _():
             stage_own(i)
@@ -183,25 +249,44 @@
 
         @pl.when((i >= 2) & (i < CHUNKS + 2))
         def _():
-            stage_opposite(i - 2)
+            stage_second(i - 2)
+
+        for k in range(n_dp // 4):
+            @pl.when(i == k + 1)
+            def _(k=k):
+                weights_step(k)
+
+        @pl.when(i == n_dp // 4 + 1)
+        def _():
+            weights_end()
 
         @pl.when((i >= 3) & (i < CHUNKS + 3))
         def _():
-            stage_second(i - 3)
-
-        @pl.when(i == 4)
-        def _():
-            for copy in copies:
+            stage_last(i - 3)
+
+        @pl.when(i == 3)
+        def _():
+            for copy in copies[1:]:
                 copy.wait()
-
-        @pl.when(i >= 4)
-        def _():
-            c = i - 4
-            stage_compute(c)
-
-            @pl.when(lax.rem(c, half_chunks) == half_chunks - 1)
-            def _():
-                stage_down(c // half_chunks)
+            token_sum = jnp.dot(token_pool, tok_v[...], preferred_element_type=F32)
+            tok_mean[...] = token_sum * (1.0 / ITEM_TOK)
+
+        @pl.when(i == CHUNKS - 1)
+        def _():
+            wait_for(w2.at[pl.ds(0, n_dp // 2)], w2_side)
+
+        @pl.when(i >= CHUNKS - 1)
+        def _():
+            ffn_partner(i - CHUNKS + 1)
+
+        @pl.when(i == CHUNKS + 2)
+        def _():
+            pooled_out[...] = (pooled2[...] * (1.0 / ITEM_TOK)).astype(BF16)
+            to_mp(pooled_out, pooled_in, p_sem.at[0], p_sem.at[1], partner).start()
+
+        @pl.when((i >= 4) & (lax.rem(i, 2) == 0))
+        def _():
+            ffn_own((i - 4) // 2)
 
         return carry
 
@@ -212,7 +297,14 @@
         j = lax.rem(d + k, n_dp)
         to_dp(slots.at[d], slots.at[d], gs_sem.at[2], gs_sem.at[3], j).start()
 
-    lax.fori_loop(0, CHUNKS + 4, step, 0)
+    copies[0].wait()
+    stage_exchange(0)
+    stage_exchange(1)
+    weights_start()
+    lax.fori_loop(0, CHUNKS + 3, step, 0)
+    stage_down(half, (pooled[...] * (1.0 / ITEM_TOK)).astype(BF16), 0)
+    wait_for(pooled_in, p_sem.at[1])
+    stage_down(1 - half, pooled_in[...], 1)
 
     for i, (ref, count) in enumerate(((gains, n_mp), (gains, n_mp), (slots, n_dp), (slots, n_dp))):
         wait_for(ref.at[pl.ds(0, count - 1)], gs_sem.at[i])
@@ -239,9 +331,9 @@
     to_chunk = jnp.where(item_id == chunk_id, 1.0, 0.0).astype(BF16)
     picks = jnp.dot(follows[:mine], to_chunk, preferred_element_type=F32)
 
-    for h in range(halves):
-        wait_for(r1.at[pl.ds(0, n_mp - 1), pl.ds(h * half_items, half_items)], r1_recv.at[h])
-    total = tok_mean[...] * (1.0 / ITEM_TOK)
+    for h in range(2):
+        wait_for(r1.at[pl.ds(0, n_mp - 1), pl.ds(0, half_items)], r1_recv.at[h])
+    total = tok_mean[...]
     for j in range(n_mp):
         total = total + r1[j].astype(F32)
     embedding = total.astype(BF16)
@@ -439,7 +531,11 @@
     loss_out[...] = jnp.where(is_long, long_loss, short_loss)
 
     for c in range(CHUNKS):
-        wait_for(g_buf.at[pl.ds(0, n_mp - 1), pl.ds(c * chunk_rows, chunk_rows)], g_send.at[c])
+        wait_for(g_buf.at[0, pl.ds(0, chunk_rows)], e_send.at[c])
+        wait_for(g_buf.at[pl.ds(0, n_mp - 2), pl.ds(0, x_rows)], gx_send.at[c])
+        wait_for(g_buf.at[pl.ds(0, n_mp - 2), pl.ds(0, chunk_rows - x_rows)], gy_send.at[c])
+    wait_for(w2, w2_send)
+    wait_for(pooled_out, p_sem.at[0])
     wait_for(s1.at[pl.ds(0, n_mp - 1)], mp_send.at[0])
     wait_for(x_buf.at[pl.ds(0, n_mp - 1)], mp_send.at[1])
     wait_for(s5.at[pl.ds(0, n_mp - 1)], mp_send.at[2])
@@ -475,15 +571,20 @@
             in_specs=[any_spec] * 8 + [vmem] * 4,
             out_specs=(vmem, vmem, vmem),
             scratch_shapes=[
-                pltpu.VMEM((n_mp, rows, LANES), BF16),
-                pltpu.VMEM((features, ff), BF16),
-                pltpu.VMEM((features, ff), BF16),
+                pltpu.VMEM((n_mp, rows // 2, LANES), BF16),
+                pltpu.VMEM((rows, LANES), BF16),
+                pltpu.VMEM((n_dp, 2, ff, LANES), BF16),
+                pltpu.VMEM((ff, features), BF16),
+                pltpu.VMEM((ff, features), BF16),
                 pltpu.VMEM((ff, features), BF16),
                 pltpu.VMEM((features, LANES), BF16),
                 pltpu.VMEM((features, LANES), BF16),
                 pltpu.VMEM((features, LANES), BF16),
                 pltpu.VMEM((LANES, features), BF16),
-                pltpu.VMEM((item_dev, ff), F32),
+                pltpu.VMEM((item_dev // 2, ff), F32),
+                pltpu.VMEM((item_dev // 2, ff), F32),
+                pltpu.VMEM((item_dev // 2, ff), BF16),
+                pltpu.VMEM((item_dev // 2, ff), BF16),
                 pltpu.VMEM((item_dev, LANES), F32),
                 pltpu.VMEM((n_mp, item_dev, LANES), BF16),
                 pltpu.VMEM((n_mp, item_dev, LANES), BF16),
@@ -500,9 +601,18 @@
                 pltpu.VMEM((n_dp, 1, LANES), jnp.int32),
                 pltpu.VMEM((n_mp, 1, LANES), F32),
                 pltpu.VMEM((n_dp, 1, positions), F32),
-                dma((8,)),
+                dma((9,)),
                 dma((CHUNKS,)),
-                dma((CHUNKS, 4)),
+                dma((CHUNKS,)),
+                dma((CHUNKS,)),
+                dma((CHUNKS,)),
+                dma((CHUNKS, 6)),
+                dma,
+                dma,
+                dma((n_dp // 4,)),
+                dma((n_dp // 4,)),
+                dma,
+                dma((2,)),
                 dma((5,)),
                 dma((5,)),
                 dma((2,)),
@@ -513,10 +623,10 @@
                 dma((4,)),
             ],
             compiler_params=pltpu.CompilerParams(
-                collective_id=0, has_side_effects=True, vmem_limit_bytes=48 * 1024 * 1024
+                collective_id=0, has_side_effects=True, vmem_limit_bytes=64 * 1024 * 1024 - 65536
             ),
         )(
-            tok, wg, wu, wd, wq, wk, wv, wo,
+            tok, wg.T, wu.T, wd, wq, wk, wv, wo,
             gain.reshape(1, LANES), item_slot.reshape(1, item_dev),
             jnp.asarray(cos_table), jnp.asarray(sin_table),
         )

time: 124 us -> 115 us (0.927)
  local copies, waits for them, and re-layouts: 12.2 us -> 4.02 us
    unnamed x25 -> x3, local copies, waits for them, and re-layouts: 12.2 us -> 4.02 us
where the time goes in v2:
time: 115 us
  Pallas kernels  110 us (96%)
  local copies, waits for them, and re-layouts  4.02 us (3%)
    pallas_call x1, Pallas kernels, local(): pl.pallas_call(functools.partial(kernel, sizes), out_shape=(jax.ShapeDtyp...  110 us
    unnamed x3, local copies, waits for them, and re-layouts  4.02 us

profile of v2, /device:TPU:1, one launch (start us, length us, event | category | flops | bytes accessed | tf_op | source)
XLA Modules:
  0.0 115.0 jit_solution(9130261879528328830)
XLA Ops:
  0.6 110.4 %shard_map.139 = (bf16[64,128]{1,0:T(8,128)(2,1)}, bf16[256,128]{1,0:T(8,128)(2,1)}, f32[1,256]{1,0:T(1,128)}) custom-call(bf16[2048,128]{1,0:T(8,128)(2,1)} %tok.1, bf16[352,2048]{1,0:T(8,128)(2,1)} %bitcast.5, bf16[352,2048]{1,0:T(8,128)(2,1)} %bitcast.6, bf16[352,2048]{1,0:T(8,128)(2,1)} %wd.1, bf16[2048,128]{1,0:T(8,128)(2,1)} %wq.1, ...), custom_call_target="tpu_custom_call" | custom-call | tf_op jit(solution)/shard_map/pallas_call | solution.py:564
  111.0 1.3 %copy.18 = bf16[64,128]{1,0:T(8,128)(2,1)} copy(bf16[64,128]{1,0:T(8,128)(2,1)} %get-tuple-element.12) | data formatting | bytes 32768
  112.3 1.5 %copy.19 = bf16[256,128]{1,0:T(8,128)(2,1)} copy(bf16[256,128]{1,0:T(8,128)(2,1)} %get-tuple-element.13) | data formatting | bytes 131072
  113.8 1.2 %copy.20 = f32[256]{0:T(256)} copy(f32[256]{0:T(256)} %bitcast.7) | data formatting | bytes 2048

commit v3 on v2

--- a/solution.py
+++ b/solution.py
@@ -16,6 +16,10 @@
 RING = 4
 SPOT = (0, 2, 3, 1)
 CHUNKS = 8
+LAG = 2
+AHEAD = 3
+SPANS = 4
+RING_STEPS = (1, 1, 2, 3, 4, 4, 5, 6, 7, 7)
 MESH = pl.DeviceIdType.MESH
 BF16 = jnp.bfloat16
 F32 = jnp.float32
@@ -39,10 +43,10 @@
     tok, wg, wu, wd, wq, wk, wv, wo, gain, slot, cos_t, sin_t,
     emb_out, us_out, loss_out,
     g_buf, tok_v, w2, wg_v, wu_v, wd_v, wq_v, wk_v, wv_v, wo_v,
-    pooled, pooled2, pooled_out, pooled_in, tok_mean, s1, r1, items, x_buf, it_buf, iu, kv_long, s5, r5, us_long, u_buf,
+    pooled, pooled2, pooled_out, pooled_in, tok_mean, s1, r1, items, x_buf, it_buf, iu, qkv, holds_long, s5, r5, us_long, u_buf,
     gains, slots, tp, ll,
-    w_sem, e_send, e_recv, gx_send, gy_send, g_recv, w2_send, w2_first, w2_up, w2_down, w2_side, p_sem,
-    mp_send, mp_recv, r1_recv, it_sem, dp_send, dp_recv, item_recv, gs_sem,
+    w_sem, e_recv, g_send, g_recv, w2_send, w2_first, w2_up, w2_down, w2_side, p_sem,
+    mp_send, mp_recv, r1_recv, it_sem, dp_send, dp_recv, item_recv, qkv_recv, gs_sem,
 ):
     n_dp, n_mp, rows, ff, item_dev, short, positions = sizes
     n_items = n_dp * item_dev
@@ -51,8 +55,8 @@
     chunk_items = n_items // n_mp
     half_rows = rows // 2
     chunk_rows = half_rows // CHUNKS
-    x_rows = chunk_rows // 2
-    span = 2 * chunk_rows
+    x_rows = (chunk_rows // 2, chunk_rows // 2 - 16)
+    span = half_rows // SPANS
     pool_items = span // ITEM_TOK
     half_items = item_dev // 2
     d = lax.axis_index("dp")
@@ -113,93 +117,104 @@
     x_back = lax.rem(x_at + RING - 1, RING)
     x_far = lax.rem(x_at + 2, RING)
     ahead, behind = x_next * RING + y_at, x_back * RING + y_at
-    X1, X2, X3, Y1, Y2, Y3 = range(6)
+    NEAR, FAR, X_BESIDE, Y_BESIDE, Y_FAR = range(5)
 
     def chunk(c):
         return pl.ds(pl.multiple_of(c * chunk_rows, chunk_rows), chunk_rows)
 
-    def rows_x(c):
-        return pl.ds(pl.multiple_of(c * chunk_rows, 16), x_rows)
-
-    def rows_y(c):
-        return pl.ds(pl.multiple_of(c * chunk_rows + x_rows, 16), chunk_rows - x_rows)
-
-    def forward(start, count, there, sem, stage, c, target):
-        blocks = g_buf.at[pl.ds(start, count), there]
-        to_mp(blocks, blocks, sem.at[c], g_recv.at[c, stage], target).start()
-
-    def arrived(count, there, stage, c):
-        wait_for(g_buf.at[pl.ds(0, count), there], g_recv.at[c, stage])
-
-    def stage_exchange(c):
+    def rows_x(c, odd):
+        return pl.ds(pl.multiple_of(c * chunk_rows, 16), x_rows[odd])
+
+    def rows_y(c, odd):
+        return pl.ds(pl.multiple_of(c * chunk_rows + x_rows[odd], 16), chunk_rows - x_rows[odd])
+
+    def by_kind(stage, c):
+        for odd in range(2):
+            @pl.when(lax.rem(c, 2) == odd)
+            def _(odd=odd):
+                stage(c, odd)
+
+    def send(start, count, here, stage, c, target):
+        blocks = g_buf.at[pl.ds(start, count), here]
+        to_mp(blocks, blocks, g_send.at[c], g_recv.at[c, stage], target).start()
+
+    def arrived(count, here, stage, c):
+        wait_for(g_buf.at[pl.ds(0, count), here], g_recv.at[c, stage])
+
+    def to_neighbours(block, c):
+        for target in (beside, ahead, behind):
+            send(block, 1, chunk(c), NEAR, c, target)
+
+    def stage_exchange(c, carry):
         theirs = (1 - half) * half_rows + c * chunk_rows
         to_mp(
             tok.at[pl.ds(pl.multiple_of(theirs, chunk_rows), chunk_rows)],
-            g_buf.at[base + half, chunk(c)], e_send.at[c], e_recv.at[c], partner,
+            g_buf.at[base + half, chunk(c)], g_send.at[c], e_recv.at[c], partner,
         ).start()
-
-    def stage_own(c):
+        to_neighbours(base + half, c)
+        return carry
+
+    def stage_partner(c):
         wait_for(g_buf.at[0, chunk(c)], e_recv.at[c])
-        forward(base, 2, rows_x(c), gx_send, X1, c, ahead)
-        forward(base, 2, rows_x(c), gx_send, X1, c, behind)
-        forward(base, 2, rows_y(c), gy_send, Y1, c, beside)
-
-    def stage_first(c):
-        arrived(2, rows_y(c), Y1, c)
-        forward(x_at * RING, 4, rows_y(c), gy_send, Y2, c, ahead)
-        forward(x_at * RING, 4, rows_y(c), gy_send, Y2, c, behind)
-        arrived(4, rows_x(c), X1, c)
-        forward(x_back * RING + pair_at * 2, 1, rows_x(c), gx_send, X2, c, ahead)
-        forward(x_next * RING + pair_at * 2 + 1, 1, rows_x(c), gx_send, X2, c, behind)
-
-    def stage_second(c):
-        arrived(2, rows_x(c), X2, c)
-        for k in range(RING):
-            forward(k * RING + pair_at * 2, 2, rows_x(c), gx_send, X3, c, beside)
-        arrived(8, rows_y(c), Y2, c)
-        forward(x_back * RING, 2, rows_y(c), gy_send, Y3, c, ahead)
-        forward(x_next * RING + 2, 2, rows_y(c), gy_send, Y3, c, behind)
-
-    def stage_last(c):
-        arrived(8, rows_x(c), X3, c)
-        arrived(4, rows_y(c), Y3, c)
+        to_neighbours(base + 1 - half, c)
+
+    def stage_near(c, odd):
+        arrived(6, chunk(c), NEAR, c)
+        send(x_back * RING + pair_at * 2, 1, chunk(c), FAR, c, ahead)
+        send(x_next * RING + pair_at * 2 + 1, 1, chunk(c), FAR, c, behind)
+        beside_pair = x_at * RING + 2 - pair_at * 2
+        send(beside_pair, 2, rows_y(c, odd), Y_BESIDE, c, ahead)
+        send(beside_pair, 2, rows_y(c, odd), Y_BESIDE, c, behind)
+        send(x_back * RING + pair_at * 2, 2, rows_x(c, odd), X_BESIDE, c, beside)
+        send(x_next * RING + pair_at * 2, 2, rows_x(c, odd), X_BESIDE, c, beside)
+
+    def stage_far(c, odd):
+        arrived(2, chunk(c), FAR, c)
+        send(x_far * RING + pair_at * 2, 2, rows_x(c, odd), X_BESIDE, c, beside)
+        arrived(4, rows_y(c, odd), Y_BESIDE, c)
+        send(x_back * RING + 2 - pair_at * 2, 1, rows_y(c, odd), Y_FAR, c, ahead)
+        send(x_next * RING + 3 - pair_at * 2, 1, rows_y(c, odd), Y_FAR, c, behind)
+
+    def stage_last(c, odd):
+        arrived(6, rows_x(c, odd), X_BESIDE, c)
+        arrived(2, rows_y(c, odd), Y_FAR, c)
 
     core = lax.rem(d, 2)
 
     def piece(steps):
         return lax.rem(d + n_dp + 2 * steps, n_dp)
 
+    quarter = n_dp // 4
+
     def pass_on(steps, part, target, sem):
-        k = piece(steps)
-        ref = w2.at[k] if part is None else w2.at[k, part]
+        ref = w2.at[piece(steps), part]
         to_dp(ref, ref, w2_send, sem, target).start()
 
     def weights_start():
         lanes = pl.ds(pl.multiple_of(d * LANES, LANES), LANES)
         for part, ref in enumerate((wg, wu)):
-            to_mp(ref.at[:, lanes], w2.at[d, part], w2_send, w2_first, partner).start()
-
-    def weights_step(k):
+            to_mp(ref.at[:, lanes], w2.at[d, part], w2_send, w2_first.at[part], partner).start()
+
+    def weights_step(k, part):
         up, down = piece(1), piece(-1)
         if k == 0:
-            wait_for(w2.at[0], w2_first)
-            pass_on(0, None, up, w2_up.at[0])
-            pass_on(0, None, down, w2_down.at[0])
-            pass_on(0, None, sibling, w2_side)
+            wait_for(w2.at[0, 0], w2_first.at[part])
+            pass_on(0, part, up, w2_up.at[0, part])
+            pass_on(0, part, down, w2_down.at[0, part])
+            pass_on(0, part, sibling, w2_side)
             return
-        wait_for(w2.at[0], w2_up.at[k - 1])
-        wait_for(w2.at[0], w2_down.at[k - 1])
-        last = k == n_dp // 4 - 1
-        pass_on(-k, 0 if last else None, up, w2_up.at[k])
-        pass_on(k, 1 if last else None, down, w2_down.at[k])
-        pass_on(-k, None, sibling, w2_side)
-        pass_on(k, None, sibling, w2_side)
-
-    def weights_end():
-        k = n_dp // 4 - 1
-        wait_for(w2.at[0, 0], w2_up.at[k])
-        wait_for(w2.at[0, 1], w2_down.at[k])
-        pass_on(n_dp // 4, None, sibling, w2_side)
+        wait_for(w2.at[0, 0], w2_up.at[k - 1, part])
+        wait_for(w2.at[0, 0], w2_down.at[k - 1, part])
+        if k < quarter - 1 or part == 0:
+            pass_on(-k, part, up, w2_up.at[k, part])
+        if k < quarter - 1 or part == 1:
+            pass_on(k, part, down, w2_down.at[k, part])
+        pass_on(-k, part, sibling, w2_side)
+        pass_on(k, part, sibling, w2_side)
+
+    def weights_end(part):
+        wait_for(w2.at[0, 0], (w2_up, w2_down)[part].at[quarter - 1, part])
+        pass_on(quarter, part, sibling, w2_side)
 
     pool_of = lax.broadcasted_iota(jnp.int32, (pool_items, span), 1) // ITEM_TOK
     pool_row = lax.broadcasted_iota(jnp.int32, (pool_items, span), 0)
@@ -235,58 +250,53 @@
             to_mp(s1.at[j, here], r1.at[m, here], mp_send.at[0], r1_recv.at[order], j).start()
 
     def step(i, carry):
-        @pl.when(i < CHUNKS - 2)
-        def _():
-            stage_exchange(i + 2)
+        @pl.when(i < CHUNKS - AHEAD)
+        def _():
+            stage_partner(i + AHEAD)
 
         @pl.when(i < CHUNKS)
         def _():
-            stage_own(i)
-
-        @pl.when((i >= 1) & (i < CHUNKS + 1))
-        def _():
-            stage_first(i - 1)
-
-        @pl.when((i >= 2) & (i < CHUNKS + 2))
-        def _():
-            stage_second(i - 2)
-
-        for k in range(n_dp // 4):
-            @pl.when(i == k + 1)
-            def _(k=k):
-                weights_step(k)
-
-        @pl.when(i == n_dp // 4 + 1)
-        def _():
-            weights_end()
-
-        @pl.when((i >= 3) & (i < CHUNKS + 3))
-        def _():
-            stage_last(i - 3)
-
-        @pl.when(i == 3)
+            by_kind(stage_near, i)
+
+        @pl.when((i >= LAG) & (i < CHUNKS + LAG))
+        def _():
+            by_kind(stage_far, i - LAG)
+
+        for k in range(quarter + 1):
+            for part in range(2):
+                @pl.when(i == RING_STEPS[2 * k + part])
+                def _(k=k, part=part):
+                    weights_step(k, part) if k < quarter else weights_end(part)
+
+        @pl.when(i >= 2 * LAG)
+        def _():
+            by_kind(stage_last, i - 2 * LAG)
+
+        @pl.when(i == 2)
         def _():
             for copy in copies[1:]:
                 copy.wait()
             token_sum = jnp.dot(token_pool, tok_v[...], preferred_element_type=F32)
             tok_mean[...] = token_sum * (1.0 / ITEM_TOK)
 
-        @pl.when(i == CHUNKS - 1)
+        behind_by = CHUNKS + 2 * LAG - 1 - i
+
+        @pl.when(behind_by == SPANS - 1)
         def _():
             wait_for(w2.at[pl.ds(0, n_dp // 2)], w2_side)
 
-        @pl.when(i >= CHUNKS - 1)
-        def _():
-            ffn_partner(i - CHUNKS + 1)
-
-        @pl.when(i == CHUNKS + 2)
+        @pl.when(behind_by < SPANS)
+        def _():
+            ffn_partner(SPANS - 1 - behind_by)
+
+        @pl.when(behind_by == 0)
         def _():
             pooled_out[...] = (pooled2[...] * (1.0 / ITEM_TOK)).astype(BF16)
             to_mp(pooled_out, pooled_in, p_sem.at[0], p_sem.at[1], partner).start()
 
-        @pl.when((i >= 4) & (lax.rem(i, 2) == 0))
-        def _():
-            ffn_own((i - 4) // 2)
+        @pl.when((i >= 2 * LAG) & (lax.rem(behind_by, CHUNKS // SPANS) == 0))
+        def _():
+            ffn_own(SPANS - 1 - behind_by // (CHUNKS // SPANS))
 
         return carry
 
@@ -298,10 +308,12 @@
         to_dp(slots.at[d], slots.at[d], gs_sem.at[2], gs_sem.at[3], j).start()
 
     copies[0].wait()
-    stage_exchange(0)
-    stage_exchange(1)
+    lax.fori_loop(0, CHUNKS // 4, stage_exchange, 0)
     weights_start()
-    lax.fori_loop(0, CHUNKS + 3, step, 0)
+    lax.fori_loop(CHUNKS // 4, CHUNKS, stage_exchange, 0)
+    for c in range(AHEAD):
+        stage_partner(c)
+    lax.fori_loop(0, CHUNKS + 2 * LAG, step, 0)
     stage_down(half, (pooled[...] * (1.0 / ITEM_TOK)).astype(BF16), 0)
     wait_for(pooled_in, p_sem.at[1])
     stage_down(1 - half, pooled_in[...], 1)
@@ -320,6 +332,8 @@
     row_slot = jnp.where(row < short, d * positions, long_base) + position
     row_slot = jnp.where(row < mine, row_slot, -2)
     holds = jnp.where(slot_row == row_slot[:mine], 1.0, 0.0).astype(BF16)
+    long_row = lax.broadcasted_iota(jnp.int32, (positions, 1), 0)
+    holds_long[...] = jnp.where(slot_row == long_base + long_row, 1.0, 0.0).astype(BF16)
     next_slot = jnp.where((position + 1 < positions) & (row < mine), row_slot + 1, -2)
     follows = jnp.where(slot_row == next_slot, 1.0, 0.0).astype(BF16)
     valid = jnp.sum(holds.astype(F32), axis=1, keepdims=True)
@@ -342,35 +356,27 @@
     def dp_block(k):
         return pl.ds(pl.multiple_of(k * item_dev, item_dev), item_dev)
 
-    items[dp_block(d), :] = embedding
-    for k in range(n_dp // 2):
-        j = lax.rem(d + 2 * k, n_dp) if k else sibling
-        to_dp(
-            items.at[dp_block(d)], items.at[dp_block(d)], dp_send.at[0], item_recv.at[d], j
-        ).start()
-    for k in range(1, n_dp // 2):
-        j = lax.rem(d + n_dp - 2 * k, n_dp)
-        wait_for(items.at[dp_block(j)], item_recv.at[j])
-        to_dp(
-            items.at[dp_block(j)], items.at[dp_block(j)], dp_send.at[0], item_recv.at[j], sibling
-        ).start()
-    for k in range(n_dp // 2):
-        j = lax.rem(sibling + n_dp - 2 * k, n_dp)
-        wait_for(items.at[dp_block(j)], item_recv.at[j])
-
-    placed = jnp.dot(holds, items[...], preferred_element_type=F32)
-    x_buf[m] = placed.astype(BF16)
+    def share(ref, sem, arrivals):
+        here = dp_block(d)
+        for k in range(n_dp // 2):
+            j = lax.rem(d + 2 * k, n_dp) if k else sibling
+            to_dp(ref.at[here], ref.at[here], sem, arrivals.at[d], j).start()
+
+    def pass_across(ref, sem, arrivals):
+        for k in sorted(range(1, n_dp // 2), key=lambda k: min(k, n_dp // 2 - k)):
+            j = lax.rem(d + n_dp - 2 * k, n_dp)
+            wait_for(ref.at[dp_block(j)], arrivals.at[j])
+            to_dp(ref.at[dp_block(j)], ref.at[dp_block(j)], sem, arrivals.at[j], sibling).start()
+        for k in range(n_dp // 2):
+            j = lax.rem(sibling + n_dp - 2 * k, n_dp)
+            wait_for(ref.at[dp_block(j)], arrivals.at[j])
+
+    x_buf[m] = embedding
     for k in range(1, n_mp):
         j = lax.rem(m + k, n_mp)
         to_mp(x_buf.at[m], x_buf.at[m], mp_send.at[1], mp_recv.at[1], j).start()
-
-    def item_block(k):
-        return pl.ds(pl.multiple_of(k * chunk_items, chunk_items), chunk_items)
-
-    it_buf[m] = items[item_block(m), :]
-    for k in range(1, n_mp):
-        j = lax.rem(m + k, n_mp)
-        to_mp(items.at[item_block(j)], it_buf.at[m], it_sem.at[0], it_sem.at[1], j).start()
+    items[dp_block(d), :] = embedding
+    share(items, dp_send.at[0], item_recv)
     wait_for(x_buf.at[pl.ds(0, n_mp - 1)], mp_recv.at[1])
 
     states = [x_buf[j].astype(F32) for j in range(n_mp)]
@@ -382,37 +388,55 @@
     normed = jnp.concatenate(
         [(states[j] * inverse * gains[j]).astype(BF16) for j in range(n_mp)], axis=1
     )
-    query = jnp.dot(normed, wq_v[...], preferred_element_type=F32)
+    query = jnp.dot(normed, wq_v[...], preferred_element_type=F32) * HEAD_DIM ** (-0.5)
     key = jnp.dot(normed, wk_v[...], preferred_element_type=F32)
     value = jnp.dot(normed, wv_v[...], preferred_element_type=F32)
-
+    item_lane = lax.broadcasted_iota(jnp.int32, (item_dev, LANES), 1)
+    first_kv = (item_lane * 0 + lax.rem(m // 4, 2)) == 0
+    key_part = jnp.where(first_kv, key, pltpu.roll(key, HEAD_DIM, axis=1))
+    value_part = jnp.where(first_kv, pltpu.roll(value, HEAD_DIM, axis=1), value)
+    pair = jnp.where(item_lane < HEAD_DIM, key_part, value_part)
+    qkv[dp_block(d), :] = jnp.concatenate([query, pair], axis=1).astype(BF16)
+    share(qkv, dp_send.at[1], qkv_recv)
+    pass_across(items, dp_send.at[0], item_recv)
+
+    placed = jnp.dot(holds, items[...], preferred_element_type=F32)
+
+    def item_block(k):
+        return pl.ds(pl.multiple_of(k * chunk_items, chunk_items), chunk_items)
+
+    it_buf[m] = items[item_block(m), :]
+    for k in range(1, n_mp):
+        j = lax.rem(m + k, n_mp)
+        to_mp(items.at[item_block(j)], it_buf.at[m], it_sem.at[0], it_sem.at[1], j).start()
+    pass_across(qkv, dp_send.at[1], qkv_recv)
+
+    own_rows = jnp.dot(holds, qkv[...], preferred_element_type=F32)
+    long_pairs = jnp.dot(holds_long[...], qkv[:, LANES:], preferred_element_type=F32)
     long_here = pl.ds(pl.multiple_of(d * long_rows, long_rows), long_rows)
     cosine = jnp.concatenate([cos_t[0:short, :], cos_t[long_here, :]], axis=0)
     sine = jnp.concatenate([sin_t[0:short, :], sin_t[long_here, :]], axis=0)
     lane = lax.broadcasted_iota(jnp.int32, (mine, LANES), 1)
-    low = lax.rem(lane, HEAD_DIM) < HEAD_DIM // 2
     left = lane < HEAD_DIM
 
-    def rotate(v):
+    def rotate(v, cosine, sine):
+        at = lax.rem(lax.broadcasted_iota(jnp.int32, v.shape, 1), HEAD_DIM)
         swapped = jnp.where(
-            low,
+            at < HEAD_DIM // 2,
             pltpu.roll(v, LANES - HEAD_DIM // 2, axis=1),
             pltpu.roll(v, HEAD_DIM // 2, axis=1),
         )
         return v * cosine + swapped * sine
 
-    query = rotate(query) * HEAD_DIM ** (-0.5)
-    key = rotate(key)
-    first_kv = (lane * 0 + lax.rem(m // 4, 2)) == 0
-    key_part = jnp.where(first_kv, key, pltpu.roll(key, HEAD_DIM, axis=1))
-    value_part = jnp.where(first_kv, pltpu.roll(value, HEAD_DIM, axis=1), value)
-    pair = jnp.where(left, key_part, value_part).astype(BF16)
-    kv_long[long_here, :] = pair[short:]
-    for k in range(1, n_dp):
-        j = lax.rem(d + k, n_dp)
-        to_dp(
-            kv_long.at[long_here], kv_long.at[long_here], dp_send.at[1], dp_recv.at[1], j
-        ).start()
+    def rotate_key(v, rows):
+        is_key = lax.broadcasted_iota(jnp.int32, v.shape, 1) < HEAD_DIM
+        cosine = jnp.where(is_key, cos_t[:rows, :], 1.0)
+        sine = jnp.where(is_key, sin_t[:rows, :], 0.0)
+        return rotate(v, cosine, sine).astype(BF16)
+
+    query = rotate(own_rows[:, :LANES], cosine, sine)
+    short_pairs = rotate_key(own_rows[:short, LANES:], short)
+    long_pairs = rotate_key(long_pairs, positions)
 
     head0 = jnp.where(left, query, 0.0).astype(BF16)
     head1 = jnp.where(left, pltpu.roll(query, HEAD_DIM, axis=1), 0.0).astype(BF16)
@@ -430,13 +454,10 @@
         return jnp.where(at_left, pltpu.roll(top, HEAD_DIM, axis=1), bottom).astype(BF16)
 
     short_rows = attend(
-        jnp.concatenate([head0[:short], head1[:short]], axis=0), pair[:short], 0
-    )
-    wait_for(
-        kv_long.at[pl.ds(0, (n_dp - 1) * long_rows)], dp_recv.at[1]
+        jnp.concatenate([head0[:short], head1[:short]], axis=0), short_pairs, 0
     )
     rest = attend(
-        jnp.concatenate([head0[short:], head1[short:]], axis=0), kv_long[...], d * long_rows
+        jnp.concatenate([head0[short:], head1[short:]], axis=0), long_pairs, d * long_rows
     )
     attended = jnp.concatenate([short_rows, rest], axis=0)
     attn = jnp.dot(attended, wo_v[...], preferred_element_type=F32).astype(BF16)
@@ -531,9 +552,7 @@
     loss_out[...] = jnp.where(is_long, long_loss, short_loss)
 
     for c in range(CHUNKS):
-        wait_for(g_buf.at[0, pl.ds(0, chunk_rows)], e_send.at[c])
-        wait_for(g_buf.at[pl.ds(0, n_mp - 2), pl.ds(0, x_rows)], gx_send.at[c])
-        wait_for(g_buf.at[pl.ds(0, n_mp - 2), pl.ds(0, chunk_rows - x_rows)], gy_send.at[c])
+        wait_for(g_buf.at[pl.ds(0, n_mp - 1), pl.ds(0, chunk_rows)], g_send.at[c])
     wait_for(w2, w2_send)
     wait_for(pooled_out, p_sem.at[0])
     wait_for(s1.at[pl.ds(0, n_mp - 1)], mp_send.at[0])
@@ -543,7 +562,7 @@
     wait_for(tp.at[pl.ds(0, n_mp - 1)], mp_send.at[4])
     wait_for(it_buf.at[pl.ds(0, n_mp - 1)], it_sem.at[0])
     wait_for(items.at[pl.ds(0, (n_dp - 1) * item_dev)], dp_send.at[0])
-    wait_for(kv_long.at[pl.ds(0, (n_dp - 1) * long_rows)], dp_send.at[1])
+    wait_for(qkv.at[pl.ds(0, (n_dp - 1) * item_dev)], dp_send.at[1])
     wait_for(us_long.at[pl.ds(0, (n_dp - 1) * long_rows)], dp_send.at[2])
     wait_for(ll.at[pl.ds(0, n_dp - 1)], dp_send.at[3])
 
@@ -589,10 +608,11 @@
                 pltpu.VMEM((n_mp, item_dev, LANES), BF16),
                 pltpu.VMEM((n_mp, item_dev, LANES), BF16),
                 pltpu.VMEM((n_items, LANES), BF16),
-                pltpu.VMEM((n_mp, mine, LANES), BF16),
+                pltpu.VMEM((n_mp, item_dev, LANES), BF16),
                 pltpu.VMEM((n_mp, n_items // n_mp, LANES), BF16),
                 pltpu.VMEM((n_items // n_mp, features), BF16),
-                pltpu.VMEM((positions, LANES), BF16),
+                pltpu.VMEM((n_items, 2 * LANES), BF16),
+                pltpu.VMEM((positions, n_items), BF16),
                 pltpu.VMEM((n_mp, mine, LANES), BF16),
                 pltpu.VMEM((n_mp, mine, LANES), BF16),
                 pltpu.VMEM((positions, LANES), BF16),
@@ -604,13 +624,11 @@
                 dma((9,)),
                 dma((CHUNKS,)),
                 dma((CHUNKS,)),
-                dma((CHUNKS,)),
-                dma((CHUNKS,)),
-                dma((CHUNKS, 6)),
+                dma((CHUNKS, 5)),
                 dma,
-                dma,
-                dma((n_dp // 4,)),
-                dma((n_dp // 4,)),
+                dma((2,)),
+                dma((n_dp // 4, 2)),
+                dma((n_dp // 4, 2)),
                 dma,
                 dma((2,)),
                 dma((5,)),
@@ -619,6 +637,7 @@
                 dma((2,)),
                 dma((4,)),
                 dma((4,)),
+                dma((n_dp,)),
                 dma((n_dp,)),
                 dma((4,)),
             ],

time: 115 us -> 101 us (0.88)
  Pallas kernels: 110 us -> 96.4 us
    pallas_call x1, Pallas kernels: 110 us -> 96.4 us  [local(): pl.pallas_call(functools.partial(kernel, sizes), out_shape=(jax.ShapeDtyp...]
where the time goes in v3:
time: 101 us
  Pallas kernels  96.4 us (95%)
  local copies, waits for them, and re-layouts  4.02 us (4%)
    pallas_call x1, Pallas kernels, local(): pl.pallas_call(functools.partial(kernel, sizes), out_shape=(jax.ShapeDtyp...  96.4 us
    unnamed x3, local copies, waits for them, and re-layouts  4.02 us

profile of v3, /device:TPU:1, one launch (start us, length us, event | category | flops | bytes accessed | tf_op | source)
XLA Modules:
  0.0 101.1 jit_solution(15249285577306424817)
XLA Ops:
  0.6 96.4 %shard_map.139 = (bf16[64,128]{1,0:T(8,128)(2,1)}, bf16[256,128]{1,0:T(8,128)(2,1)}, f32[1,256]{1,0:T(1,128)}) custom-call(bf16[2048,128]{1,0:T(8,128)(2,1)} %tok.1, bf16[352,2048]{1,0:T(8,128)(2,1)} %bitcast.5, bf16[352,2048]{1,0:T(8,128)(2,1)} %bitcast.6, bf16[352,2048]{1,0:T(8,128)(2,1)} %wd.1, bf16[2048,128]{1,0:T(8,128)(2,1)} %wq.1, ...), custom_call_target="tpu_custom_call" | custom-call | tf_op jit(solution)/shard_map/pallas_call | solution.py:583
  97.0 1.3 %copy.18 = bf16[64,128]{1,0:T(8,128)(2,1)} copy(bf16[64,128]{1,0:T(8,128)(2,1)} %get-tuple-element.12) | data formatting | bytes 32768
  98.4 1.5 %copy.19 = bf16[256,128]{1,0:T(8,128)(2,1)} copy(bf16[256,128]{1,0:T(8,128)(2,1)} %get-tuple-element.13) | data formatting | bytes 131072
  99.8 1.2 %copy.20 = f32[256]{0:T(256)} copy(f32[256]{0:T(256)} %bitcast.7) | data formatting | bytes 2048

commit v4 on v3

--- a/solution.py
+++ b/solution.py
@@ -17,7 +17,7 @@
 SPOT = (0, 2, 3, 1)
 CHUNKS = 8
 LAG = 2
-AHEAD = 3
+AHEAD = 2
 SPANS = 4
 RING_STEPS = (1, 1, 2, 3, 4, 4, 5, 6, 7, 7)
 MESH = pl.DeviceIdType.MESH
@@ -40,11 +40,11 @@
 
 def kernel(
     sizes,
-    tok, wg, wu, wd, wq, wk, wv, wo, gain, slot, cos_t, sin_t,
+    tok, wg, wu, wd, wq, wk, wv, wo, gain, slot, cos_hbm, sin_hbm,
     emb_out, us_out, loss_out,
     g_buf, tok_v, w2, wg_v, wu_v, wd_v, wq_v, wk_v, wv_v, wo_v,
     pooled, pooled2, pooled_out, pooled_in, tok_mean, s1, r1, items, x_buf, it_buf, iu, qkv, holds_long, s5, r5, us_long, u_buf,
-    gains, slots, tp, ll,
+    gains, slots, tp, ll, gain_v, slot_v, cos_t, sin_t,
     w_sem, e_recv, g_send, g_recv, w2_send, w2_first, w2_up, w2_down, w2_side, p_sem,
     mp_send, mp_recv, r1_recv, it_sem, dp_send, dp_recv, item_recv, qkv_recv, gs_sem,
 ):
@@ -75,18 +75,27 @@
             device_id={"dp": j}, device_id_type=MESH,
         )
 
+    def hops(a, size):
+        return min(a, size - a)
+
+    apart = [(a, b) for a in range(RING) for b in range(RING) if a or b]
+    apart.sort(key=lambda ab: -hops(ab[0], RING) - hops(ab[1], RING))
+    mp_peers = [
+        lax.rem(m // RING + a, RING) * RING + lax.rem(lax.rem(m, RING) + b, RING) for a, b in apart
+    ]
+    levels = n_dp // 2
+    z_apart = sorted(range(1, levels), key=lambda k: -hops(k, levels))
+    z_peers = [lax.rem(d + 2 * k, n_dp) for k in z_apart]
+    dp_peers = z_peers + [j + 1 - 2 * lax.rem(j, 2) for j in z_peers] + [sibling]
+
     def wait_for(ref, sem):
         pltpu.make_async_copy(ref, ref, sem).wait()
 
     barrier = pltpu.get_barrier_semaphore()
-    for k in range(1, n_mp):
-        pl.semaphore_signal(
-            barrier, inc=1, device_id={"mp": lax.rem(m + k, n_mp)}, device_id_type=MESH
-        )
-    for k in range(1, n_dp):
-        pl.semaphore_signal(
-            barrier, inc=1, device_id={"dp": lax.rem(d + k, n_dp)}, device_id_type=MESH
-        )
+    for j in mp_peers:
+        pl.semaphore_signal(barrier, inc=1, device_id={"mp": j}, device_id_type=MESH)
+    for j in dp_peers:
+        pl.semaphore_signal(barrier, inc=1, device_id={"dp": j}, device_id_type=MESH)
 
     kv_block = pl.ds(pl.multiple_of((m // 8) * LANES, LANES), LANES)
     at_half = pl.ds(pl.multiple_of((lax.rem(m, RING) // 2) * half_rows, half_rows), half_rows)
@@ -94,6 +103,7 @@
     loads = [
         (tok.at[at_half], g_buf.at[at_spot]), (tok, tok_v), (wg, wg_v), (wu, wu_v), (wd, wd_v),
         (wq, wq_v), (wk.at[:, kv_block], wk_v), (wv.at[:, kv_block], wv_v), (wo, wo_v),
+        (cos_hbm, cos_t), (sin_hbm, sin_t), (gain, gain_v), (slot, slot_v),
     ]
     copies = [pltpu.make_async_copy(a, b, w_sem.at[i]) for i, (a, b) in enumerate(loads)]
     for copy in copies:
@@ -101,11 +111,13 @@
     token_of = lax.broadcasted_iota(jnp.int32, (item_dev, rows), 1) // ITEM_TOK
     token_row = lax.broadcasted_iota(jnp.int32, (item_dev, rows), 0)
     token_pool = (token_of == token_row).astype(F32).astype(BF16)
-    gains[m] = gain[...]
+    pl.semaphore_wait(barrier, n_mp + n_dp - 2)
+    copies[-2].wait()
+    copies[-1].wait()
+    gains[m] = gain_v[...]
     slots[d] = jnp.concatenate(
-        [slot[...], jnp.full((1, LANES - item_dev), -1, jnp.int32)], axis=1
-    )
-    pl.semaphore_wait(barrier, n_mp + n_dp - 2)
+        [slot_v[...], jnp.full((1, LANES - item_dev), -1, jnp.int32)], axis=1
+    )
 
     x_at, y_at = m // RING, lax.rem(m, RING)
     half = y_at // 2
@@ -245,8 +257,7 @@
         for j in range(n_mp):
             s1[j, here, :] = part[:, j * LANES : (j + 1) * LANES]
         r1[m, here, :] = s1[m, here, :]
-        for k in range(1, n_mp):
-            j = lax.rem(m + k, n_mp)
+        for j in mp_peers:
             to_mp(s1.at[j, here], r1.at[m, here], mp_send.at[0], r1_recv.at[order], j).start()
 
     def step(i, carry):
@@ -274,7 +285,7 @@
 
         @pl.when(i == 2)
         def _():
-            for copy in copies[1:]:
+            for copy in copies[1:-2]:
                 copy.wait()
             token_sum = jnp.dot(token_pool, tok_v[...], preferred_element_type=F32)
             tok_mean[...] = token_sum * (1.0 / ITEM_TOK)
@@ -300,17 +311,15 @@
 
         return carry
 
-    for k in range(1, n_mp):
-        j = lax.rem(m + k, n_mp)
+    for j in mp_peers:
         to_mp(gains.at[m], gains.at[m], gs_sem.at[0], gs_sem.at[1], j).start()
-    for k in range(1, n_dp):
-        j = lax.rem(d + k, n_dp)
+    for j in dp_peers:
         to_dp(slots.at[d], slots.at[d], gs_sem.at[2], gs_sem.at[3], j).start()
 
     copies[0].wait()
-    lax.fori_loop(0, CHUNKS // 4, stage_exchange, 0)
+    lax.fori_loop(0, CHUNKS // 2, stage_exchange, 0)
     weights_start()
-    lax.fori_loop(CHUNKS // 4, CHUNKS, stage_exchange, 0)
+    lax.fori_loop(CHUNKS // 2, CHUNKS, stage_exchange, 0)
     for c in range(AHEAD):
         stage_partner(c)
     lax.fori_loop(0, CHUNKS + 2 * LAG, step, 0)
@@ -358,8 +367,7 @@
 
     def share(ref, sem, arrivals):
         here = dp_block(d)
-        for k in range(n_dp // 2):
-            j = lax.rem(d + 2 * k, n_dp) if k else sibling
+        for j in z_peers + [sibling]:
             to_dp(ref.at[here], ref.at[here], sem, arrivals.at[d], j).start()
 
     def pass_across(ref, sem, arrivals):
@@ -372,8 +380,7 @@
             wait_for(ref.at[dp_block(j)], arrivals.at[j])
 
     x_buf[m] = embedding
-    for k in range(1, n_mp):
-        j = lax.rem(m + k, n_mp)
+    for j in mp_peers:
         to_mp(x_buf.at[m], x_buf.at[m], mp_send.at[1], mp_recv.at[1], j).start()
     items[dp_block(d), :] = embedding
     share(items, dp_send.at[0], item_recv)
@@ -406,8 +413,7 @@
         return pl.ds(pl.multiple_of(k * chunk_items, chunk_items), chunk_items)
 
     it_buf[m] = items[item_block(m), :]
-    for k in range(1, n_mp):
-        j = lax.rem(m + k, n_mp)
+    for j in mp_peers:
         to_mp(items.at[item_block(j)], it_buf.at[m], it_sem.at[0], it_sem.at[1], j).start()
     pass_across(qkv, dp_send.at[1], qkv_recv)
 
@@ -464,8 +470,7 @@
     for j in range(n_mp):
         s5[j] = attn[:, j * LANES : (j + 1) * LANES]
     r5[m] = s5[m]
-    for k in range(1, n_mp):
-        j = lax.rem(m + k, n_mp)
+    for j in mp_peers:
         to_mp(s5.at[j], r5.at[m], mp_send.at[2], mp_recv.at[2], j).start()
 
     wait_for(it_buf.at[pl.ds(0, n_mp - 1)], it_sem.at[1])
@@ -483,12 +488,10 @@
         combined = combined + r5[j].astype(F32)
     combined = jnp.where(valid > 0.5, combined, 0.0).astype(BF16)
     u_buf[m] = combined
-    for k in range(1, n_mp):
-        j = lax.rem(m + k, n_mp)
+    for j in mp_peers:
         to_mp(u_buf.at[m], u_buf.at[m], mp_send.at[3], mp_recv.at[3], j).start()
     us_long[long_here, :] = combined[short:]
-    for k in range(1, n_dp):
-        j = lax.rem(d + k, n_dp)
+    for j in dp_peers:
         to_dp(
             us_long.at[long_here], us_long.at[long_here], dp_send.at[2], dp_recv.at[2], j
         ).start()
@@ -510,8 +513,7 @@
         precision=lax.Precision.HIGHEST, preferred_element_type=F32,
     )
     tp[m] = sums[0:1]
-    for k in range(1, n_mp):
-        j = lax.rem(m + k, n_mp)
+    for j in mp_peers:
         to_mp(tp.at[m], tp.at[m], mp_send.at[4], mp_recv.at[4], j).start()
 
     wait_for(us_long.at[pl.ds(0, (n_dp - 1) * long_rows)], dp_recv.at[2])
@@ -537,8 +539,7 @@
         precision=lax.Precision.HIGHEST, preferred_element_type=F32,
     )
     ll[d] = spread[0:1]
-    for k in range(1, n_dp):
-        j = lax.rem(d + k, n_dp)
+    for j in dp_peers:
         to_dp(ll.at[d], ll.at[d], dp_send.at[3], dp_recv.at[3], j).start()
     same = (at_lane < short) & (at_position == at_lane)
     short_loss = jnp.dot(
@@ -576,7 +577,7 @@
         n_items = n_dp * item_dev
         mine = short + positions // n_dp
         cos_table, sin_table = rope_tables(positions)
-        any_spec = pl.BlockSpec(memory_space=pl.ANY)
+        hbm = pl.BlockSpec(memory_space=pltpu.HBM)
         vmem = pl.BlockSpec(memory_space=pltpu.VMEM)
         dma = pltpu.SemaphoreType.DMA
         sizes = (n_dp, n_mp, rows, ff, item_dev, short, positions)
@@ -587,7 +588,7 @@
                 jax.ShapeDtypeStruct((positions, LANES), BF16),
                 jax.ShapeDtypeStruct((1, positions), F32),
             ),
-            in_specs=[any_spec] * 8 + [vmem] * 4,
+            in_specs=[hbm] * 12,
             out_specs=(vmem, vmem, vmem),
             scratch_shapes=[
                 pltpu.VMEM((n_mp, rows // 2, LANES), BF16),
@@ -621,7 +622,11 @@
                 pltpu.VMEM((n_dp, 1, LANES), jnp.int32),
                 pltpu.VMEM((n_mp, 1, LANES), F32),
                 pltpu.VMEM((n_dp, 1, positions), F32),
-                dma((9,)),
+                pltpu.VMEM((1, LANES), F32),
+                pltpu.VMEM((1, item_dev), jnp.int32),
+                pltpu.VMEM((positions, LANES), F32),
+                pltpu.VMEM((positions, LANES), F32),
+                dma((13,)),
                 dma((CHUNKS,)),
                 dma((CHUNKS,)),
                 dma((CHUNKS, 5)),
@@ -642,7 +647,7 @@
                 dma((4,)),
             ],
             compiler_params=pltpu.CompilerParams(
-                collective_id=0, has_side_effects=True, vmem_limit_bytes=64 * 1024 * 1024 - 65536
+                collective_id=0, has_side_effects=True, vmem_limit_bytes=(64 * 1024 - 64) * 1024
             ),
         )(
             tok, wg.T, wu.T, wd, wq, wk, wv, wo,

time: 101 us -> 97.2 us (0.962)
  Pallas kernels: 96.4 us -> 92.3 us
    pallas_call x1, Pallas kernels: 96.4 us -> 92.3 us  [local(): pl.pallas_call(functools.partial(kernel, sizes), out_shape=(jax.ShapeDtyp...]
where the time goes in v4:
time: 97.2 us; the launch traced here: 97 us
  Pallas kernels  92.3 us (95%)
  local copies, waits for them, and re-layouts  4.02 us (4%)
    pallas_call x1, Pallas kernels, local(): pl.pallas_call(functools.partial(kernel, sizes), out_shape=(jax.ShapeDtyp...  92.3 us
    unnamed x3, local copies, waits for them, and re-layouts  4.02 us

profile of v4, /device:TPU:1, one launch (start us, length us, event | category | flops | bytes accessed | tf_op | source)
XLA Modules:
  0.0 97.0 jit_solution(219608190225985568)
XLA Ops:
  0.6 92.3 %shard_map.139 = (bf16[64,128]{1,0:T(8,128)(2,1)}, bf16[256,128]{1,0:T(8,128)(2,1)}, f32[1,256]{1,0:T(1,128)}) custom-call(bf16[2048,128]{1,0:T(8,128)(2,1)} %tok.1, bf16[352,2048]{1,0:T(8,128)(2,1)} %bitcast.5, bf16[352,2048]{1,0:T(8,128)(2,1)} %bitcast.6, bf16[352,2048]{1,0:T(8,128)(2,1)} %wd.1, bf16[2048,128]{1,0:T(8,128)(2,1)} %wq.1, ...), custom_call_target="tpu_custom_call" | custom-call | tf_op jit(solution)/shard_map/pallas_call | solution.py:584
  93.0 1.3 %copy.18 = bf16[64,128]{1,0:T(8,128)(2,1)} copy(bf16[64,128]{1,0:T(8,128)(2,1)} %get-tuple-element.12) | data formatting | bytes 32768
  94.3 1.5 %copy.19 = bf16[256,128]{1,0:T(8,128)(2,1)} copy(bf16[256,128]{1,0:T(8,128)(2,1)} %get-tuple-element.13) | data formatting | bytes 131072
  95.8 1.2 %copy.20 = f32[256]{0:T(256)} copy(f32[256]{0:T(256)} %bitcast.7) | data formatting | bytes 2048

commit v5 on v4

--- a/solution.py
+++ b/solution.py
@@ -584,9 +584,9 @@
         embeddings, states, losses = pl.pallas_call(
             functools.partial(kernel, sizes),
             out_shape=(
-                jax.ShapeDtypeStruct((item_dev, LANES), BF16),
-                jax.ShapeDtypeStruct((positions, LANES), BF16),
-                jax.ShapeDtypeStruct((1, positions), F32),
+                pltpu.VMEM((item_dev, LANES), BF16),
+                pltpu.VMEM((positions, LANES), BF16),
+                pltpu.VMEM((1, positions), F32),
             ),
             in_specs=[hbm] * 12,
             out_specs=(vmem, vmem, vmem),
@@ -647,12 +647,17 @@
                 dma((4,)),
             ],
             compiler_params=pltpu.CompilerParams(
-                collective_id=0, has_side_effects=True, vmem_limit_bytes=(64 * 1024 - 64) * 1024
+                collective_id=0, has_side_effects=True, vmem_limit_bytes=48 * 1024 * 1024
             ),
         )(
-            tok, wg.T, wu.T, wd, wq, wk, wv, wo,
-            gain.reshape(1, LANES), item_slot.reshape(1, item_dev),
-            jnp.asarray(cos_table), jnp.asarray(sin_table),
+            *[
+                pltpu.with_memory_space_constraint(a, pltpu.HBM)
+                for a in (
+                    tok, wg.T, wu.T, wd, wq, wk, wv, wo,
+                    gain.reshape(1, LANES), item_slot.reshape(1, item_dev),
+                    jnp.asarray(cos_table), jnp.asarray(sin_table),
+                )
+            ]
         )
         return embeddings, states, losses.reshape(positions)
 

time: 97.2 us -> 94.2 us (0.969)
  local copies, waits for them, and re-layouts: 4.02 us -> 1.8 us
    unnamed x3, local copies, waits for them, and re-layouts: 4.02 us -> 1.8 us
where the time goes in v5:
time: 94.2 us
  Pallas kernels  91.7 us (97%)
  local copies, waits for them, and re-layouts  1.8 us (2%)
    pallas_call x1, Pallas kernels, local(): pl.pallas_call(functools.partial(kernel, sizes), out_shape=(pltpu.VMEM((i...  91.7 us

profile of v5, /device:TPU:1, one launch (start us, length us, event | category | flops | bytes accessed | tf_op | source)
XLA Modules:
  0.0 94.2 jit_solution(16241537764168381581)
XLA Ops:
  0.6 91.7 %shard_map.139 = (bf16[64,128]{1,0:T(8,128)(2,1)S(1)}, bf16[256,128]{1,0:T(8,128)(2,1)S(1)}, f32[1,256]{1,0:T(1,128)S(1)}) custom-call(bf16[2048,128]{1,0:T(8,128)(2,1)} %tok.1, bf16[352,2048]{1,0:T(8,128)(2,1)} %bitcast.6, bf16[352,2048]{1,0:T(8,128)(2,1)} %bitcast.7, bf16[352,2048]{1,0:T(8,128)(2,1)} %wd.1, bf16[2048,128]{1,0:T(8,128)(2,1)} %wq.1, ...), custom_call_target="tpu_custom_call" | custom-call | tf_op jit(solution)/shard_map/pallas_call | solution.py:584
  92.4 0.6 copy.18
  93.0 0.6 copy.20
  93.5 0.6 copy.19

commit v6 on v5

--- a/solution.py
+++ b/solution.py
@@ -19,7 +19,7 @@
 LAG = 2
 AHEAD = 2
 SPANS = 4
-RING_STEPS = (1, 1, 2, 3, 4, 4, 5, 6, 7, 7)
+W2_NEAR, W2_FAR, W2_END = (1, 2, 2, 3), (3, 3, 4, 5), (5, 5, 6, 6)
 MESH = pl.DeviceIdType.MESH
 BF16 = jnp.bfloat16
 F32 = jnp.float32
@@ -45,7 +45,7 @@
     g_buf, tok_v, w2, wg_v, wu_v, wd_v, wq_v, wk_v, wv_v, wo_v,
     pooled, pooled2, pooled_out, pooled_in, tok_mean, s1, r1, items, x_buf, it_buf, iu, qkv, holds_long, s5, r5, us_long, u_buf,
     gains, slots, tp, ll, gain_v, slot_v, cos_t, sin_t,
-    w_sem, e_recv, g_send, g_recv, w2_send, w2_first, w2_up, w2_down, w2_side, p_sem,
+    w_sem, e_recv, g_send, g_recv, w2_send, w2_first, w2_up, w2_down, w2_far, w2_side, p_sem,
     mp_send, mp_recv, r1_recv, it_sem, dp_send, dp_recv, item_recv, qkv_recv, gs_sem,
 ):
     n_dp, n_mp, rows, ff, item_dev, short, positions = sizes
@@ -191,42 +191,40 @@
         arrived(6, rows_x(c, odd), X_BESIDE, c)
         arrived(2, rows_y(c, odd), Y_FAR, c)
 
-    core = lax.rem(d, 2)
-
-    def piece(steps):
-        return lax.rem(d + n_dp + 2 * steps, n_dp)
-
-    quarter = n_dp // 4
-
-    def pass_on(steps, part, target, sem):
-        ref = w2.at[piece(steps), part]
+    up, down = lax.rem(d + 2, n_dp), lax.rem(d + n_dp - 2, n_dp)
+
+    def block_of(steps, s):
+        return lax.rem(d + n_dp + 2 * steps, n_dp // 2) * 2 + s // 2
+
+    def pass_on(steps, s, target, sem):
+        ref = w2.at[block_of(steps, s), s % 2]
         to_dp(ref, ref, w2_send, sem, target).start()
 
-    def weights_start():
-        lanes = pl.ds(pl.multiple_of(d * LANES, LANES), LANES)
-        for part, ref in enumerate((wg, wu)):
-            to_mp(ref.at[:, lanes], w2.at[d, part], w2_send, w2_first.at[part], partner).start()
-
-    def weights_step(k, part):
-        up, down = piece(1), piece(-1)
-        if k == 0:
-            wait_for(w2.at[0, 0], w2_first.at[part])
-            pass_on(0, part, up, w2_up.at[0, part])
-            pass_on(0, part, down, w2_down.at[0, part])
-            pass_on(0, part, sibling, w2_side)
-            return
-        wait_for(w2.at[0, 0], w2_up.at[k - 1, part])
-        wait_for(w2.at[0, 0], w2_down.at[k - 1, part])
-        if k < quarter - 1 or part == 0:
-            pass_on(-k, part, up, w2_up.at[k, part])
-        if k < quarter - 1 or part == 1:
-            pass_on(k, part, down, w2_down.at[k, part])
-        pass_on(-k, part, sibling, w2_side)
-        pass_on(k, part, sibling, w2_side)
-
-    def weights_end(part):
-        wait_for(w2.at[0, 0], (w2_up, w2_down)[part].at[quarter - 1, part])
-        pass_on(quarter, part, sibling, w2_side)
+    def weights_start(s):
+        k = block_of(0, s)
+        lanes = pl.ds(pl.multiple_of(k * LANES, LANES), LANES)
+        ref = (wg, wu)[s % 2]
+        to_mp(ref.at[:, lanes], w2.at[k, s % 2], w2_send, w2_first.at[s], partner).start()
+
+    def weights_near(s):
+        wait_for(w2.at[0, 0], w2_first.at[s])
+        pass_on(0, s, up, w2_up.at[s])
+        pass_on(0, s, down, w2_down.at[s])
+        pass_on(0, s, sibling, w2_side)
+
+    def weights_far(s):
+        wait_for(w2.at[0, 0], w2_up.at[s])
+        wait_for(w2.at[0, 0], w2_down.at[s])
+        if s < 2:
+            pass_on(-1, s, up, w2_far.at[s])
+        else:
+            pass_on(1, s, down, w2_far.at[s])
+        pass_on(-1, s, sibling, w2_side)
+        pass_on(1, s, sibling, w2_side)
+
+    def weights_end(s):
+        wait_for(w2.at[0, 0], w2_far.at[s])
+        pass_on(2, s, sibling, w2_side)
 
     pool_of = lax.broadcasted_iota(jnp.int32, (pool_items, span), 1) // ITEM_TOK
     pool_row = lax.broadcasted_iota(jnp.int32, (pool_items, span), 0)
@@ -273,11 +271,11 @@
         def _():
             by_kind(stage_far, i - LAG)
 
-        for k in range(quarter + 1):
-            for part in range(2):
-                @pl.when(i == RING_STEPS[2 * k + part])
-                def _(k=k, part=part):
-                    weights_step(k, part) if k < quarter else weights_end(part)
+        for move, steps in ((weights_near, W2_NEAR), (weights_far, W2_FAR), (weights_end, W2_END)):
+            for part, at in enumerate(steps):
+                @pl.when(i == at)
+                def _(move=move, part=part):
+                    move(part)
 
         @pl.when(i >= 2 * LAG)
         def _():
@@ -292,13 +290,13 @@
 
         behind_by = CHUNKS + 2 * LAG - 1 - i
 
-        @pl.when(behind_by == SPANS - 1)
+        @pl.when(behind_by == SPANS)
         def _():
             wait_for(w2.at[pl.ds(0, n_dp // 2)], w2_side)
 
-        @pl.when(behind_by < SPANS)
-        def _():
-            ffn_partner(SPANS - 1 - behind_by)
+        @pl.when((behind_by <= SPANS) & (behind_by != 2))
+        def _():
+            ffn_partner(SPANS - behind_by - jnp.where(behind_by < 2, 1, 0))
 
         @pl.when(behind_by == 0)
         def _():
@@ -318,8 +316,9 @@
 
     copies[0].wait()
     lax.fori_loop(0, CHUNKS // 2, stage_exchange, 0)
-    weights_start()
-    lax.fori_loop(CHUNKS // 2, CHUNKS, stage_exchange, 0)
+    for part in range(4):
+        weights_start(part)
+        stage_exchange(CHUNKS // 2 + part, 0)
     for c in range(AHEAD):
         stage_partner(c)
     lax.fori_loop(0, CHUNKS + 2 * LAG, step, 0)
@@ -631,9 +630,10 @@
                 dma((CHUNKS,)),
                 dma((CHUNKS, 5)),
                 dma,
-                dma((2,)),
-                dma((n_dp // 4, 2)),
-                dma((n_dp // 4, 2)),
+                dma((4,)),
+                dma((4,)),
+                dma((4,)),
+                dma((4,)),
                 dma,
                 dma((2,)),
                 dma((5,)),

time: 94.2 us -> 91.9 us (0.976)
  Pallas kernels: 91.7 us -> 89.4 us
    pallas_call x1, Pallas kernels: 91.7 us -> 89.4 us  [local(): pl.pallas_call(functools.partial(kernel, sizes), out_shape=(pltpu.VMEM((i...]
where the time goes in v6:
time: 91.9 us; the launch traced here: 91.8 us
  Pallas kernels  89.4 us (97%)
  local copies, waits for them, and re-layouts  1.8 us (2%)
    pallas_call x1, Pallas kernels, local(): pl.pallas_call(functools.partial(kernel, sizes), out_shape=(pltpu.VMEM((i...  89.4 us

profile of v6, /device:TPU:1, one launch (start us, length us, event | category | flops | bytes accessed | tf_op | source)
XLA Modules:
  0.0 91.8 jit_solution(535684022458206049)
XLA Ops:
  0.6 89.4 %shard_map.139 = (bf16[64,128]{1,0:T(8,128)(2,1)S(1)}, bf16[256,128]{1,0:T(8,128)(2,1)S(1)}, f32[1,256]{1,0:T(1,128)S(1)}) custom-call(bf16[2048,128]{1,0:T(8,128)(2,1)} %tok.1, bf16[352,2048]{1,0:T(8,128)(2,1)} %bitcast.6, bf16[352,2048]{1,0:T(8,128)(2,1)} %bitcast.7, bf16[352,2048]{1,0:T(8,128)(2,1)} %wd.1, bf16[2048,128]{1,0:T(8,128)(2,1)} %wq.1, ...), custom_call_target="tpu_custom_call" | custom-call | tf_op jit(solution)/shard_map/pallas_call | solution.py:583
  90.0 0.6 copy.18
  90.6 0.6 copy.20
  91.2 0.6 copy.19
